TPU v7x, 256 devices: a whole 4x4x8 slice. The times are simulated.
256 devices in a mesh: op: 16 (over x, y), tm: 16 (over z, core).
Axes of the slice: x: 4, y: 4, z: 8, core: 2. Of those that a mesh axis runs over, the one named last changes fastest.
Arguments:
- elementals: bfloat16 [128, 32, 256, 256], P('op', 'tm'), may hold values from -6 to 6
- perambulators: bfloat16 [32, 4, 256, 256], P('tm'), may hold values from -0.375 to 0.375
- src_times: int32 [4], replicated, may hold values from 0 to 31, as said below
- pair_ops: int32 [2048, 2], replicated, may hold values from 0 to 127, as said below
- conj_flags: int32 [2048], replicated, may hold values 0 or 1
Outputs:
- correlator: float32 [2048, 32, 4], P('op', 'tm')
Inputs may be any that keep to these rules, and one draw needn't show every extreme that they name: `src_times`: the 4 entries are different timeslices, one of them the last. `pair_ops`: the two operators of a pair have equal numbers modulo 4.
All inputs are finite; a program needn't handle non-finite values.
Results may differ from a plain program's by a relative error of at most 0.0041.
Values may be sent and summed in bfloat16 or wider, within the bound.
No kernel may reach another device: no remote copies, remote signals or barrier semaphores. Data moves between devices by JAX's collectives and lax.ppermute only.
A program may use at most 128 MiB of HBM per device.

v0:
```python
import jax
import jax.numpy as jnp
from jax import lax
from jax.sharding import PartitionSpec as P

IRREPS = 4


def from_root(block, axis, source):
    block = jnp.where(lax.axis_index(axis) == source, block, jnp.zeros_like(block))
    return lax.psum(block, axis)


def per_device(elementals, perambulators, src_times, pair_ops, conj_flags):
    op_dev, sink_count, mode_count, _ = elementals.shape
    source_count = perambulators.shape[1]
    holder = src_times // sink_count
    within = src_times % sink_count
    gathered = []
    for source_idx in range(source_count):
        picked = lax.dynamic_index_in_dim(elementals, within[source_idx], 1, keepdims=False)
        gathered.append(from_root(picked, "tm", holder[source_idx]))
    stacked = jnp.stack(gathered, 1)
    source_cols = lax.all_to_all(stacked, "op", split_axis=2, concat_axis=0, tiled=True)
    half_product = jnp.einsum(
        "atij,tkjl->taikl", elementals, perambulators, preferred_element_type=jnp.float32
    ).astype(jnp.bfloat16)
    sandwich = jnp.einsum(
        "tkji,tajkl->tkial", perambulators, half_product, preferred_element_type=jnp.float32
    ).astype(jnp.bfloat16)
    left_ops = pair_ops[:, 0]
    right_ops = pair_ops[:, 1]
    mirrored = conj_flags[:, None, None] == 1
    columns = lax.all_to_all(sandwich, "op", split_axis=2, concat_axis=3, tiled=True)
    times_here, src_here, row_share, ops_total, col_count = columns.shape
    groups = ops_total // IRREPS
    grouped = columns.reshape(times_here, src_here, row_share, groups, IRREPS, col_count)
    source_grouped = source_cols.reshape(groups, IRREPS, src_here, row_share, col_count)
    products = jnp.einsum(
        "tkigrl,hrkil->tkrgh", grouped, source_grouped, preferred_element_type=jnp.float32
    )
    left_class = left_ops % IRREPS
    forward = products[:, :, left_class, left_ops // IRREPS, right_ops // IRREPS]
    backward = products[:, :, left_class, right_ops // IRREPS, left_ops // IRREPS]
    forward = jnp.transpose(forward, (2, 0, 1))
    backward = jnp.transpose(backward, (2, 0, 1))
    symmetric = jnp.where(mirrored, 0.5 * (forward + backward), forward)
    partial_value = symmetric / mode_count
    return lax.psum_scatter(partial_value, "op", scatter_dimension=0, tiled=True)


def solution(mesh):
    return jax.shard_map(
        per_device,
        mesh=mesh,
        in_specs=(P("op", "tm", None, None), P("tm", None, None, None), P(), P(), P()),
        out_specs=P("op", "tm", None),
        check_vma=False,
    )
```

profile of v0, /device:TPU:1, one launch (start us, length us, event | category | flops | bytes accessed | tf_op | source)
XLA Modules:
  0.0 612.6 jit_solution(5232350023756177117)
XLA Ops:
  6.5 0.8 and_select_fusion.3
  7.3 0.7 fusion.25
  18.1 2.6 constant_dynamic-slice_fusion.3
  20.7 3.5 broadcast_select_fusion
  24.3 3.5 broadcast_select_fusion.1
  27.8 3.5 broadcast_select_fusion.2
  31.3 3.5 broadcast_select_fusion.3
  34.7 0.0 all-reduce.7.cloned.1.call-update
  34.8 138.0 %all-reduce.7.cloned.1.call-done = (bf16[8,1,256,256]{3,1,0,2:T(2,128)(2,1)}, bf16[8,1,256,256]{3,1,0,2:T(2,128)(2,1)}, bf16[8,1,256,256]{3,1,0,2:T(2,128)(2,1)}, bf16[8,1,256,256]{3,1,0,2:T(2,128)(2,1)}) async-done(((bf16[8,1,256,256]{3,1,0,2:T(2,128)(2,1)}, bf16[8,1,256,256]{3,1,0,2:T(2,128)(2,1)}, bf16[8,1,256,256]{3,1,0,2:T(2,128)(2,1)}, bf16[8,1,256,256]{3,1,0,2:T(2,128)(2,1)}), ...) | async-done | bytes 4194320 | tf_op jit(solution)/shard_map/psum | solution.py:11
  172.7 12.8 %pad_maximum_fusion = bf16[8,4,256,256]{3,1,0,2:T(4,128)(2,1)} fusion(bf16[8,1,256,256]{3,1,0,2:T(2,128)(2,1)} %get-tuple-element.5, bf16[8,1,256,256]{3,1,0,2:T(2,128)(2,1)} %get-tuple-element.6, bf16[8,1,256,256]{3,1,0,2:T(2,128)(2,1)} %get-tuple-element.7, bf16[8,1,256,256]{3,1,0,2:T(2,128)(2,1)} %get-tuple-element.8), kind=kLoop, calls=%fused_computation.8 | loop fusion | flops 16777216 | bytes 8388608 | tf_op jit(solution)/shard_map/stack | solution.py:23
  185.5 6.7 %all-to-all-start = ((bf16[8,4,256,256]{3,1,0,2:T(4,128)(2,1)}), bf16[8,4,256,256]{3,1,0,2:T(4,128)(2,1)}, u32[]{:S(2)}, u32[]{:S(2)}) async-start(bf16[8,4,256,256]{3,1,0,2:T(4,128)(2,1)} %pad_maximum_fusion), calls=%async_computation | async-start | bytes 8388608 | tf_op jit(solution)/shard_map/all_to_all | solution.py:24
  192.2 6.7 %convert_bitcast_fusion = bf16[2,4,256,8,256]{2,4,3,1,0:T(8,128)(2,1)} fusion(bf16[2,4,256,256]{3,2,1,0:T(8,128)(2,1)S(1)} %copy-done, bf16[8,2,256,256]{3,2,1,0:T(8,128)(2,1)S(1)} %copy-done.2), kind=kOutput, calls=%fused_computation.4 | convolution fusion | flops 4303355904 | bytes 11534336 | tf_op jit(solution)/shard_map/tkji,tajkl->tkial/dot_general | solution.py:28
  198.9 14.7 %copy.31 = bf16[2,4,256,8,256]{4,3,1,0,2:T(8,128)(2,1)} copy(bf16[2,4,256,8,256]{2,4,3,1,0:T(8,128)(2,1)} %convert_bitcast_fusion) | data formatting | bytes 16777216 | tf_op jit(solution)/shard_map/convert_element_type | solution.py:30
  213.6 29.5 %all-to-all-done = bf16[8,4,256,256]{3,1,0,2:T(4,128)(2,1)} async-done(((bf16[8,4,256,256]{3,1,0,2:T(4,128)(2,1)}), bf16[8,4,256,256]{3,1,0,2:T(4,128)(2,1)}, u32[]{:S(2)}, u32[]{:S(2)}) %all-to-all-start) | async-done | bytes 4194336 | tf_op jit(solution)/shard_map/all_to_all | solution.py:24
  243.2 5.2 all-to-all-start.1
  248.3 0.2 all-reduce.5.cloned.1.call-start
  248.6 0.2 shift-left_or_fusion
  248.8 4.6 copy.27
  253.3 2.6 copy.28
  255.9 89.8 %all-to-all-done.1 = bf16[2,4,256,8,256]{4,3,1,0,2:T(8,128)(2,1)} async-done(((bf16[2,4,256,8,256]{4,3,1,0,2:T(8,128)(2,1)}), bf16[2,4,256,8,256]{4,3,1,0,2:T(8,128)(2,1)}, u32[]{:S(2)}, u32[]{:S(2)}) %all-to-all-start.1) | async-done | bytes 8388640 | tf_op jit(solution)/shard_map/all_to_all | solution.py:34
  345.7 16.1 %copy.33 = bf16[2,4,16,16,8,256]{5,2,4,3,1,0:T(8,128)(2,1)} copy(bf16[2,4,16,16,8,256]{5,4,1,0,2,3:T(8,128)(2,1)} %bitcast.18) | data formatting | bytes 16777216 | tf_op jit(solution)/shard_map/all_to_all | solution.py:34
  361.9 18.2 %fusion.11 = f32[2,4,4,32,32]{3,4,0,2,1:T(8,128)S(1)} fusion(bf16[2,4,16,32,4,256]{5,2,4,3,1,0:T(8,128)(2,1)} %bitcast.42, bf16[32,4,4,16,256,1]{4,3,2,1,0,5:T(8,128)(2,1)S(1)} %bitcast.43), kind=kOutput, calls=%fused_computation.16 | convolution fusion | flops 268435456 | bytes 12713984 | tf_op jit(solution)/shard_map/tkigrl,hrkil->tkrgh/dot_general | solution.py:39
  380.1 5.7 copy.36
  385.9 12.8 %gather_fusion = f32[2048,2,4]{2,1,0:T(2,128)S(1)} fusion(f32[2,4,4,32,32]{1,0,4,3,2:T(2,128)} %copy.36, s32[2048]{0:T(1024)S(1)} %bitcast.40), kind=kCustom, calls=%fused_computation | custom fusion | bytes 155648 | tf_op jit(solution)/shard_map/gather | solution.py:43
  398.6 22.1 %gather_fusion.1 = f32[2048,2,4]{2,1,0:T(2,128)} fusion(f32[2,4,4,32,32]{1,0,4,3,2:T(2,128)} %copy.36, s32[2048]{0:T(1024)S(1)} %bitcast.39), kind=kCustom, calls=%fused_computation.1 | custom fusion | bytes 155648 | tf_op jit(solution)/shard_map/gather | solution.py:44
  420.7 11.1 %select_multiply_fusion = f32[2048,2,4]{2,1,0:T(2,128)} fusion(f32[2048,2,4]{2,1,0:T(2,128)S(1)} %gather_fusion, f32[2048,2,4]{2,1,0:T(2,128)} %gather_fusion.1, pred[2048]{0:T(1024)(128)(4,1)S(1)} %broadcast_compare_fusion), kind=kLoop, calls=%fused_computation.15 | loop fusion | flops 65536 | bytes 198656 | tf_op jit(solution)/shard_map/div | solution.py:48
  431.8 0.0 all-reduce.5.cloned.1.call-update
  431.9 0.6 copy-done.6
  432.5 0.6 dynamic-slice
  433.7 170.2 %all-reduce.5.cloned.1.call-done = f32[2048,2,4]{2,1,0:T(2,128)} async-done(((f32[2048,2,4]{2,1,0:T(2,128)}), f32[2048,2,4]{2,1,0:T(2,128)}) %all-reduce.5.cloned.1.call-update) | async-done | bytes 65552
  604.0 0.9 constant_dynamic-slice_fusion.4
  604.9 0.7 copy.38
  (16 shorter events, 0.1 us)
Async XLA Ops:
  6.5 185.7 %copy-start = (bf16[2,4,256,256]{3,2,1,0:T(8,128)(2,1)S(1)}, bf16[2,4,256,256]{3,2,1,0:T(8,128)(2,1)}, u32[]{:S(2)}) copy-start(bf16[2,4,256,256]{3,2,1,0:T(8,128)(2,1)} %param.6) | copy-start | bytes 3145732
  6.5 166.2 %all-reduce.7.cloned.1.call-start = ((), (), s32[]{:S(2)}) async-start(), calls=%async_computation.3 | async-start | bytes 16777216 | tf_op jit(solution)/shard_map/psum | solution.py:11
  185.5 6.7 %copy-start.2 = (bf16[8,2,256,256]{3,2,1,0:T(8,128)(2,1)S(1)}, bf16[8,2,256,256]{3,2,1,0:T(8,128)(2,1)}, u32[]{:S(2)}) copy-start(bf16[8,2,256,256]{3,2,1,0:T(8,128)(2,1)} %param.5) | copy-start | bytes 6291460
  185.5 57.6 %all-to-all-start = ((bf16[8,4,256,256]{3,1,0,2:T(4,128)(2,1)}), bf16[8,4,256,256]{3,1,0,2:T(4,128)(2,1)}, u32[]{:S(2)}, u32[]{:S(2)}) async-start(bf16[8,4,256,256]{3,1,0,2:T(4,128)(2,1)} %pad_maximum_fusion), calls=%async_computation | async-start | bytes 8388608 | tf_op jit(solution)/shard_map/all_to_all | solution.py:24
  213.6 34.9 %copy-start.5 = (s32[2048]{0:T(1024)S(1)}, s32[2048]{0:T(1024)}, u32[]{:S(2)}) copy-start(s32[2048]{0:T(1024)} %param.9) | copy-start | bytes 24580
  213.6 35.0 %copy-start.4 = (s32[2048,2]{0,1:T(2,128)S(1)}, s32[2048,2]{0,1:T(2,128)}, u32[]{:S(2)}) copy-start(s32[2048,2]{0,1:T(2,128)} %param.8) | copy-start | bytes 49156
  243.2 102.6 %all-to-all-start.1 = ((bf16[2,4,256,8,256]{4,3,1,0,2:T(8,128)(2,1)}), bf16[2,4,256,8,256]{4,3,1,0,2:T(8,128)(2,1)}, u32[]{:S(2)}, u32[]{:S(2)}) async-start(bf16[2,4,256,8,256]{4,3,1,0,2:T(8,128)(2,1)} %copy.31), calls=%async_computation.1 | async-start | bytes 16777216 | tf_op jit(solution)/shard_map/all_to_all | solution.py:34
  248.3 355.6 %all-reduce.5.cloned.1.call-start = ((), (), s32[]{:S(2)}) async-start(), calls=%async_computation.2 | async-start | bytes 4194304
  345.7 16.1 %copy-start.3 = (bf16[16,8,4,16,256]{4,3,2,1,0:T(8,128)(2,1)S(1)}, bf16[16,8,4,16,256]{4,3,2,1,0:T(8,128)(2,1)}, u32[]{:S(2)}) copy-start(bf16[16,8,4,16,256]{4,3,2,1,0:T(8,128)(2,1)} %copy.28) | copy-start | bytes 12582916
  420.7 184.8 %copy-start.1 = (bf16[2,4,256,256]{3,2,1,0:T(8,128)(2,1)S(1)}, bf16[2,4,256,256]{3,2,1,0:T(8,128)(2,1)}, u32[]{:S(2)}) copy-start(bf16[2,4,256,256]{3,2,1,0:T(8,128)(2,1)} %param.6) | copy-start | bytes 3145732
  431.8 0.7 copy-start.6
Sparse Core Ops, SparseCore 0:
  34.9 137.8 all-reduce.6
  432.0 171.9 all-reduce.4
where the time goes:
time: 621 us; the launch traced here: 613 us
  waiting for transfers between devices  428 us (69%)
  local copies, waits for them, and re-layouts  84.7 us (14%)
  other arithmetic  38.8 us (6%)
  matrix products  24.9 us (4%)
  between operations  24.5 us (4%)
  starting transfers between devices  12.1 us (2%)
    unnamed x3, waiting for transfers between devices  170 us
    psum x1, waiting for transfers between devices, from_root(): return lax.psum(block, axis)  138 us
    all_to_all x1, waiting for transfers between devices, per_device(): lax.all_to_all(sandwich, 'op', split_axis=2, concat_axis=3, tiled=True)  89.8 us
    all_to_all x1, waiting for transfers between devices, per_device(): lax.all_to_all(stacked, 'op', split_axis=2, concat_axis=0, tiled=True)  29.5 us
    gather x1, local copies, waits for them, and re-layouts, per_device(): products[:, :, left_class, right_ops // IRREPS, left_ops // IRREPS]  22.1 us
    dot_general x1, matrix products, per_device(): jnp.einsum('tkigrl,hrkil->tkrgh', grouped, source_grouped, preferred_elem...  18.2 us
    all_to_all x1, local copies, waits for them, and re-layouts, per_device(): lax.all_to_all(sandwich, 'op', split_axis=2, concat_axis=3, tiled=True)  16.1 us
    convert_element_type x1, local copies, waits for them, and re-layouts, per_device(): sandwich = jnp.einsum('tkji,tajkl->tkial', perambulators, half_product, p...  14.7 us
  transfers between devices with their start and end apart: 4, of which 4 were waited for; matrix products, arithmetic and copies ran while one was open for 5% of the time, Pallas kernels for 0%

commit v1 on v0

v1 whole, which is shorter than its diff:
```python
import jax
import jax.numpy as jnp
from jax import lax
from jax.experimental import pallas as pl
from jax.experimental.pallas import tpu as pltpu
from jax.sharding import Mesh, PartitionSpec as P

CLASSES = 4
LANES = 128
F32 = jnp.float32
BF16 = jnp.bfloat16


def shift(block, axis, step):
    size = lax.axis_size(axis)
    return lax.ppermute(block, axis, [(i, (i + step) % size) for i in range(size)])


def sandwich_kernel(e_ref, p_ref, pt_ref, w_ref, wide):
    ops, modes = e_ref.shape[0], e_ref.shape[2]
    for a in range(ops):
        half = jnp.dot(e_ref[a, 0], p_ref[0], preferred_element_type=F32).astype(BF16)
        whole = jnp.dot(pt_ref[0], half, preferred_element_type=F32)
        for part in range(modes // LANES):
            wide[part, pl.ds(a, modes, stride=ops), :] = whole[:, part * LANES : (part + 1) * LANES]
    for part in range(modes // LANES):
        w_ref[:, :, part * LANES : (part + 1) * LANES] = wide[part].reshape(modes, ops, LANES).astype(BF16)


def sandwiches(elements, props, props_t):
    ops, times, modes, _ = elements.shape
    return pl.pallas_call(
        sandwich_kernel,
        grid=(times,),
        in_specs=[
            pl.BlockSpec((ops, 1, modes, modes), lambda t: (0, t, 0, 0)),
            pl.BlockSpec((1, modes, modes), lambda t: (t, 0, 0)),
            pl.BlockSpec((1, modes, modes), lambda t: (t, 0, 0)),
        ],
        out_specs=pl.BlockSpec((modes, ops, modes), lambda t: (0, t, 0)),
        out_shape=jax.ShapeDtypeStruct((modes, times * ops, modes), BF16),
        scratch_shapes=[pltpu.VMEM((modes // LANES, modes * ops, LANES), F32)],
        compiler_params=pltpu.CompilerParams(vmem_limit_bytes=32 * 2**20),
        cost_estimate=pl.CostEstimate(
            flops=4 * ops * times * modes**3, bytes_accessed=4 * ops * times * modes**2, transcendentals=0
        ),
    )(elements, props, props_t)


def product_kernel(at_ref, wa_ref, wb_ref, s_ref, o_ref):
    rows = s_ref.shape[0]
    sources = jnp.concatenate([s_ref[r] for r in range(rows)], 1)
    for half, w_ref in enumerate((wa_ref, wb_ref)):
        left = jnp.concatenate([w_ref[r] for r in range(rows)], 1)
        o_ref[half] = lax.dot_general(left, sources, (((1,), (1,)), ((), ())), preferred_element_type=F32)


def block_products(at, near, far, sources):
    rows, count, modes = sources.shape
    left = near.shape[1]
    return pl.pallas_call(
        product_kernel,
        grid_spec=pltpu.PrefetchScalarGridSpec(
            num_scalar_prefetch=1,
            grid=(1,),
            in_specs=[
                pl.BlockSpec((rows, left, modes), lambda i, at: (at[0], 0, 0)),
                pl.BlockSpec((rows, left, modes), lambda i, at: (at[0], 0, 0)),
                pl.BlockSpec((rows, count, modes), lambda i, at: (0, 0, 0)),
            ],
            out_specs=pl.BlockSpec((2, left, count), lambda i, at: (0, 0, 0)),
        ),
        out_shape=jax.ShapeDtypeStruct((2, left, count), F32),
        compiler_params=pltpu.CompilerParams(vmem_limit_bytes=32 * 2**20),
        cost_estimate=pl.CostEstimate(
            flops=4 * rows * left * count * modes,
            bytes_accessed=2 * rows * modes * (2 * left + count),
            transcendentals=0,
        ),
    )(at.reshape(1).astype(jnp.int32), near, far, sources)


def scatter_z(chunk):
    z, size = lax.axis_index("z"), lax.axis_size("z")
    reach = size // 2
    up = down = None
    for step in range(reach):
        mine = chunk((z + size - (reach - step)) % size)
        down = shift(mine if down is None else mine + down, "z", -1)
        if step:
            mine = chunk((z + reach - step) % size)
            up = shift(mine if up is None else mine + up, "z", 1)
    return chunk(z) + up + down


def gather_z(block):
    reach = lax.axis_size("z") // 2
    found = [(0, block)]
    up = down = block
    for step in range(1, reach):
        up, down = shift(up, "z", 1), shift(down, "z", -1)
        found += [(-step, up), (step, down)]
    half = block.shape[0] // 2
    last = jnp.concatenate([shift(up[:half], "z", 1), shift(down[half:], "z", -1)], 0)
    return found + [(reach, last)]


def per_device(elementals, perambulators, src_times, pair_ops, conj_flags):
    ops, times, modes, _ = elementals.shape
    sources = perambulators.shape[1]
    z, core = lax.axis_index("z"), lax.axis_index("c")
    planes = lax.axis_size("z")
    chips = lax.axis_size("x") * lax.axis_size("y")
    place = lax.axis_index("x") * lax.axis_size("y") + lax.axis_index("y")
    k_half = place % 2
    my_k = 2 * k_half + core
    xy = ("x", "y")

    spread = jnp.broadcast_to(elementals[:, None], (ops, 2, times, modes, modes)).reshape(chips, times, modes, modes)

    beside = shift(elementals, "c", 1)
    slots = []
    for kh in range(2):
        when = src_times[2 * kh + core]
        inside = when % times
        own = lax.dynamic_index_in_dim(elementals, inside, 1, keepdims=False)
        other = lax.dynamic_index_in_dim(beside, inside, 1, keepdims=False)
        holder = when // times
        held = jnp.where(holder % 2 == core, own, other)
        slots.append(jnp.where(holder // 2 == z, held, jnp.zeros_like(held)))
    slots = jnp.stack(slots)
    rows = modes // planes
    mine = scatter_z(lambda j: lax.dynamic_slice_in_dim(slots, j * rows, rows, 2))

    spread = lax.all_to_all(spread, xy, 0, 0, tiled=True)

    mine = mine.reshape(2, 2, CLASSES, rows, modes).transpose(2, 0, 1, 3, 4)
    mine = jnp.broadcast_to(mine[None], (2,) + mine.shape).reshape(chips, 2, rows, modes)
    mine = lax.all_to_all(mine, xy, 0, 0, tiled=True)
    mine = mine.reshape(2 * chips, rows, modes).transpose(1, 0, 2)

    props_near = lax.dynamic_index_in_dim(perambulators, my_k, 1, keepdims=False)
    props_far = shift(lax.dynamic_index_in_dim(perambulators, 2 * k_half + 1 - core, 1, keepdims=False), "c", 1)
    spread_far = shift(spread, "c", 1)
    near = sandwiches(spread, props_near, jnp.swapaxes(props_near, 1, 2))
    far = sandwiches(spread_far, props_far, jnp.swapaxes(props_far, 1, 2))

    total = None
    for offset, block in gather_z(mine):
        part = block_products((z + planes + offset) % planes, near, far, block)
        total = part if total is None else total + part
    by_core = jnp.where(core == 0, total, total[::-1])
    by_core = by_core.reshape(2, 8, -1)
    out = jnp.broadcast_to(by_core[None], (chips,) + by_core.shape).reshape((2 * chips,) + by_core.shape[1:])
    out = lax.all_to_all(out, ("x", "y", "c"), 0, 0, tiled=True)
    groups = 2 * chips
    table = out.reshape(2, CLASSES, 2, 2, times, chips, groups).transpose(5, 0, 1, 4, 2, 3, 6)
    table = table.reshape(CLASSES * groups, times * sources * groups)

    pairs = pair_ops.shape[0] // chips
    local = lax.dynamic_slice_in_dim(pair_ops, place * pairs, pairs, 0)
    flags = lax.dynamic_slice_in_dim(conj_flags, place * pairs, pairs, 0)
    left, right = local[:, 0], local[:, 1]

    def picked(first, second):
        row = (first[:, None] == jnp.arange(CLASSES * groups)[None]).astype(F32)
        lines = jnp.dot(row, table, precision=lax.Precision.HIGHEST, preferred_element_type=F32)
        lines = lines.reshape(pairs, times * sources, groups)
        column = (second // CLASSES)[:, None, None] == jnp.arange(groups)[None, None]
        return jnp.sum(jnp.where(column, lines, 0.0), 2)

    forward, backward = picked(left, right), picked(right, left)
    symmetric = jnp.where(flags[:, None] == 1, 0.5 * (forward + backward), forward)
    return (symmetric / modes).reshape(pairs, times, sources)


def solution(mesh):
    chips = Mesh(mesh.devices.reshape(4, 4, 8, 2), ("x", "y", "z", "c"))
    op, tm = ("x", "y"), ("z", "c")
    return jax.shard_map(
        per_device,
        mesh=chips,
        in_specs=(P(op, tm, None, None), P(tm, None, None, None), P(), P(), P()),
        out_specs=P(op, tm, None),
        check_vma=False,
    )
```

time: 621 us -> 208 us (0.33); the launches traced: 613 us -> 208 us
  waiting for transfers between devices: 428 us -> 85.8 us
  local copies, waits for them, and re-layouts: 84.7 us -> 15 us
  starting transfers between devices: 12.1 us -> 55.8 us
  other arithmetic: 38.8 us -> 6.16 us
  matrix products: 24.9 us -> 0.64 us
  Pallas kernels: 0 us -> 20 us
  between operations: 24.5 us -> 5.41 us
  blocking collectives: 0 us -> 18.6 us
    unnamed x3 -> x0, waiting for transfers between devices: 170 us -> none
    psum x1 -> x0, waiting for transfers between devices: 138 us -> none  [from_root(): return lax.psum(block, axis)]
    all_to_all x2, waiting for transfers between devices: 119 us -> 51.3 us  [the longest x1 44.3 us: per_device(): spread = lax.all_to_all(spread, xy, 0, 0, tiled=True)]
    ppermute x0 -> x18, starting transfers between devices: none -> 36.4 us  [shift(): lax.ppermute(block, axis, [(i, (i + step) % size) for i in range(size)])]
    gather x2 -> x0, local copies, waits for them, and re-layouts: 34.9 us -> none  [the longest x1 22.1 us: per_device(): products[:, :, left_class, right_ops // IRREPS, left_ops // IRREPS]]
    ppermute x0 -> x18, waiting for transfers between devices: none -> 34.5 us  [shift(): lax.ppermute(block, axis, [(i, (i + step) % size) for i in range(size)])]
    dot_general x2, matrix products: 24.9 us -> 0.64 us  [picked(): jnp.dot(row, table, precision=lax.Precision.HIGHEST, preferred_element_ty...]
    all_to_all x3 -> x1, local copies, waits for them, and re-layouts: 23.3 us -> 0.54 us  [per_device(): mine = lax.all_to_all(mine, xy, 0, 0, tiled=True)]
  transfers between devices with their start and end apart: 4 -> 20, of which waited for: 4 -> 8; matrix products, arithmetic and copies ran while one was open for 5% -> 6% of each run, Pallas kernels for 0% -> 4%
where the time goes in v1:
time: 208 us
  waiting for transfers between devices  85.8 us (41%)
  starting transfers between devices  55.8 us (27%)
  Pallas kernels  20 us (10%)
  blocking collectives  18.6 us (9%)
  local copies, waits for them, and re-layouts  15 us (7%)
  other arithmetic  6.16 us (3%)
  between operations  5.41 us (3%)
    all_to_all x1, waiting for transfers between devices, per_device(): spread = lax.all_to_all(spread, xy, 0, 0, tiled=True)  44.3 us
    ppermute x18, starting transfers between devices, shift(): lax.ppermute(block, axis, [(i, (i + step) % size) for i in range(size)])  36.4 us
    ppermute x18, waiting for transfers between devices, shift(): lax.ppermute(block, axis, [(i, (i + step) % size) for i in range(size)])  34.5 us
    all_to_all x1, blocking collectives, per_device(): mine = lax.all_to_all(mine, xy, 0, 0, tiled=True)  18.6 us
    pallas_call x2, Pallas kernels, sandwiches(): pl.pallas_call(sandwich_kernel, grid=(times,), in_specs=[pl.BlockSpec((op...  15.4 us
    all_to_all x1, starting transfers between devices, per_device(): out = lax.all_to_all(out, ('x', 'y', 'c'), 0, 0, tiled=True)  11.6 us
    all_to_all x1, starting transfers between devices, per_device(): spread = lax.all_to_all(spread, xy, 0, 0, tiled=True)  7.77 us
    all_to_all x1, waiting for transfers between devices, per_device(): out = lax.all_to_all(out, ('x', 'y', 'c'), 0, 0, tiled=True)  7.03 us
  transfers between devices with their start and end apart: 20, of which 8 were waited for; matrix products, arithmetic and copies ran while one was open for 6% of the time, Pallas kernels for 4%

profile of v1, /device:TPU:1, one launch (start us, length us, event | category | flops | bytes accessed | tf_op | source)
XLA Modules:
  0.0 207.5 jit_solution(11842747749112017140)
XLA Ops:
  0.0 4.1 %broadcast_in_dim.54 = bf16[8,2,2,256,256]{4,3,2,1,0:T(8,128)(2,1)} broadcast(bf16[8,2,256,256]{3,2,1,0:T(8,128)(2,1)} %param.5), dimensions={0,2,3,4} | broadcast | bytes 6291456 | tf_op jit(solution)/shard_map/broadcast_in_dim | solution.py:119
  4.1 7.8 %all-to-all-start = ((bf16[16,2,256,256]{3,2,1,0:T(8,128)(2,1)}), bf16[16,2,256,256]{3,2,1,0:T(8,128)(2,1)}, u32[]{:S(2)}, u32[]{:S(2)}) async-start(bf16[16,2,256,256]{3,2,1,0:T(8,128)(2,1)} %bitcast.64), calls=%async_computation | async-start | bytes 8388608 | tf_op jit(solution)/shard_map/all_to_all | solution.py:135
  11.9 1.5 copy.30
  13.4 1.0 collective-permute-start.2
  20.0 1.5 fusion.2
  21.9 1.6 select_bitcast_fusion
  23.5 5.7 %collective-permute-start.6 = (bf16[2,8,32,256]{3,2,1,0:T(8,128)(2,1)S(1)}, bf16[2,8,32,256]{3,2,1,0:T(8,128)(2,1)S(1)}, u32[]{:S(2)}, u32[]{:S(2)}) collective-permute-start(bf16[2,8,32,256]{3,2,1,0:T(8,128)(2,1)S(1)} %fusion.3), channel_id=1, source_target_pairs={{0,14},{2,0},{4,2},{6,4},{8,6},{10,8},{12,10},{14,12},{1,15},{3,1}... | collective-permute-start | bytes 786440 | tf_op jit(solution)/shard_map/ppermute | solution.py:16
  29.1 44.3 %all-to-all-done.e_ref = bf16[16,2,256,256]{3,2,1,0:T(8,128)(2,1)} async-done(((bf16[16,2,256,256]{3,2,1,0:T(8,128)(2,1)}), bf16[16,2,256,256]{3,2,1,0:T(8,128)(2,1)}, u32[]{:S(2)}, u32[]{:S(2)}) %all-to-all-start) | async-done | bytes 4194336 | tf_op jit(solution)/shard_map/all_to_all | solution.py:135
  73.4 2.4 %collective-permute-start = (bf16[16,2,256,256]{3,2,1,0:T(8,128)(2,1)}, bf16[16,2,256,256]{3,2,1,0:T(8,128)(2,1)}, u32[]{:S(2)}, u32[]{:S(2)}) collective-permute-start(bf16[16,2,256,256]{3,2,1,0:T(8,128)(2,1)} %all-to-all-done.e_ref), channel_id=1, source_target_pairs={{0,1},{1,0},{2,3},{3,2},{4,5},{5,4},{6,7},{7,6},{8,9},{9,8},{10,11... | collective-permute-start | bytes 12582920 | tf_op jit(solution)/shard_map/ppermute | solution.py:16
  75.9 1.7 collective-permute-start.3
  77.6 4.0 %collective-permute-start.7 = (bf16[2,8,32,256]{3,2,1,0:T(8,128)(2,1)S(1)}, bf16[2,8,32,256]{3,2,1,0:T(8,128)(2,1)S(1)}, u32[]{:S(2)}, u32[]{:S(2)}) collective-permute-start(bf16[2,8,32,256]{3,2,1,0:T(8,128)(2,1)S(1)} %get-tuple-element.10), channel_id=1, source_target_pairs={{0,14},{2,0},{4,2},{6,4},{8,6},{10,8},{12,10},{14,12},{1,15},{3,1}... | collective-permute-start | bytes 786440 | tf_op jit(solution)/shard_map/ppermute | solution.py:16
  81.6 6.6 %collective-permute-done.3 = bf16[2,8,32,256]{3,2,1,0:T(8,128)(2,1)S(1)} collective-permute-done((bf16[2,8,32,256]{3,2,1,0:T(8,128)(2,1)S(1)}, bf16[2,8,32,256]{3,2,1,0:T(8,128)(2,1)S(1)}, u32[]{:S(2)}, u32[]{:S(2)}) %collective-permute-start.3) | collective-permute-done | bytes 262176 | tf_op jit(solution)/shard_map/ppermute | solution.py:16
  88.5 2.7 %collective-permute-start.8 = (bf16[2,8,32,256]{3,2,1,0:T(8,128)(2,1)S(1)}, bf16[2,8,32,256]{3,2,1,0:T(8,128)(2,1)S(1)}, u32[]{:S(2)}, u32[]{:S(2)}) collective-permute-start(bf16[2,8,32,256]{3,2,1,0:T(8,128)(2,1)S(1)} %get-tuple-element.8), channel_id=1, source_target_pairs={{0,14},{2,0},{4,2},{6,4},{8,6},{10,8},{12,10},{14,12},{1,15},{3,1}... | collective-permute-start | bytes 786440 | tf_op jit(solution)/shard_map/ppermute | solution.py:16
  91.1 5.8 %collective-permute-done.4 = bf16[2,8,32,256]{3,2,1,0:T(8,128)(2,1)S(1)} collective-permute-done((bf16[2,8,32,256]{3,2,1,0:T(8,128)(2,1)S(1)}, bf16[2,8,32,256]{3,2,1,0:T(8,128)(2,1)S(1)}, u32[]{:S(2)}, u32[]{:S(2)}) %collective-permute-start.4) | collective-permute-done | bytes 262176 | tf_op jit(solution)/shard_map/ppermute | solution.py:16
  97.1 2.4 %collective-permute-start.9 = (bf16[2,8,32,256]{3,2,1,0:T(8,128)(2,1)S(1)}, bf16[2,8,32,256]{3,2,1,0:T(8,128)(2,1)S(1)}, u32[]{:S(2)}, u32[]{:S(2)}) collective-permute-start(bf16[2,8,32,256]{3,2,1,0:T(8,128)(2,1)S(1)} %get-tuple-element.6), channel_id=1, source_target_pairs={{0,14},{2,0},{4,2},{6,4},{8,6},{10,8},{12,10},{14,12},{1,15},{3,1}... | collective-permute-start | bytes 786440 | tf_op jit(solution)/shard_map/ppermute | solution.py:16
  99.6 4.0 %collective-permute-done.9 = bf16[2,8,32,256]{3,2,1,0:T(8,128)(2,1)S(1)} collective-permute-done((bf16[2,8,32,256]{3,2,1,0:T(8,128)(2,1)S(1)}, bf16[2,8,32,256]{3,2,1,0:T(8,128)(2,1)S(1)}, u32[]{:S(2)}, u32[]{:S(2)}) %collective-permute-start.9) | collective-permute-done | bytes 262176 | tf_op jit(solution)/shard_map/ppermute | solution.py:16
  103.6 3.0 %collective-permute-done.5 = bf16[2,8,32,256]{3,2,1,0:T(8,128)(2,1)S(1)} collective-permute-done((bf16[2,8,32,256]{3,2,1,0:T(8,128)(2,1)S(1)}, bf16[2,8,32,256]{3,2,1,0:T(8,128)(2,1)S(1)}, u32[]{:S(2)}, u32[]{:S(2)}) %collective-permute-start.5) | collective-permute-done | bytes 262176 | tf_op jit(solution)/shard_map/ppermute | solution.py:16
  107.4 18.6 %all_to_all.15 = bf16[16,2,32,256]{3,1,2,0:T(2,128)(2,1)S(1)} all-to-all(bf16[16,2,32,256]{3,1,2,0:T(2,128)(2,1)S(1)} %bitcast.66), channel_id=1, replica_groups=mesh['x'=4,'y'=4,'z'=8,'c'=2] {'x','y'}, dimensions={0} | all-to-all | bytes 1048576 | tf_op jit(solution)/shard_map/all_to_all | solution.py:139
  127.1 1.2 collective-permute-start.10
  128.3 7.6 %collective-permute-done.11.s_ref = bf16[32,32,256]{2,1,0:T(8,128)(2,1)S(1)} collective-permute-done((bf16[32,32,256]{2,1,0:T(8,128)(2,1)S(1)}, bf16[32,32,256]{2,1,0:T(8,128)(2,1)S(1)}, u32[]{:S(2)}, u32[]{:S(2)}) %collective-permute-start.11) | collective-permute-done | bytes 524320 | tf_op jit(solution)/shard_map/ppermute | solution.py:16
  135.8 1.8 collective-permute-start.13
  138.5 7.6 %collective-permute-done.13.s_ref = bf16[32,32,256]{2,1,0:T(8,128)(2,1)S(1)} collective-permute-done((bf16[32,32,256]{2,1,0:T(8,128)(2,1)S(1)}, bf16[32,32,256]{2,1,0:T(8,128)(2,1)S(1)}, u32[]{:S(2)}, u32[]{:S(2)}) %collective-permute-start.13) | collective-permute-done | bytes 524320 | tf_op jit(solution)/shard_map/ppermute | solution.py:16
  146.1 1.9 collective-permute-start.15
  148.0 1.1 constant_dynamic-slice_fusion
  149.2 9.8 %collective-permute-start.1 = (bf16[2,256,256]{1,2,0:T(8,128)(2,1)S(1)}, bf16[2,256,256]{1,2,0:T(8,128)(2,1)S(1)}, u32[]{:S(2)}, u32[]{:S(2)}) collective-permute-start(bf16[2,256,256]{1,2,0:T(8,128)(2,1)S(1)} %bitcast.71), channel_id=1, source_target_pairs={{0,1},{1,0},{2,3},{3,2},{4,5},{5,4},{6,7},{7,6},{8,9},{9,8},{10,11... | collective-permute-start | bytes 786440 | tf_op jit(solution)/shard_map/ppermute | solution.py:16
  159.8 1.0 collective-permute-start.17
  162.4 7.7 %shard_map.55.wa_ref = bf16[256,32,256]{2,1,0:T(8,128)(2,1)S(1)} custom-call(bf16[16,2,256,256]{3,2,1,0:T(8,128)(2,1)} %all-to-all-done.e_ref, bf16[2,256,256]{2,1,0:T(8,128)(2,1)S(1)} %bitcast.58, bf16[2,256,256]{2,1,0:T(8,128)(2,1)S(1)} %bitcast.63), custom_call_target="tpu_custom_call" | custom-call | flops 2147483648 | bytes 8388608 | tf_op jit(solution)/shard_map/pallas_call | solution.py:32
  170.1 1.1 pad_maximum_fusion.s_ref
  171.2 7.7 %shard_map.56.wb_ref = bf16[256,32,256]{2,1,0:T(8,128)(2,1)S(1)} custom-call(bf16[16,2,256,256]{3,2,1,0:T(8,128)(2,1)} %collective-permute-done.e_ref, bf16[2,256,256]{2,1,0:T(8,128)(2,1)S(1)} %copy.29.p_ref, bf16[2,256,256]{2,1,0:T(8,128)(2,1)S(1)} %bitcast.62), custom_call_target="tpu_custom_call" | custom-call | flops 2147483648 | bytes 8388608 | tf_op jit(solution)/shard_map/pallas_call | solution.py:32
  181.8 1.5 shard_map.60
  185.6 11.6 %all-to-all-start.2 = ((f32[32,8,128]{2,1,0:T(8,128)}), f32[32,8,128]{2,1,0:T(8,128)S(1)}, u32[]{:S(2)}, u32[]{:S(2)}) async-start(f32[32,8,128]{2,1,0:T(8,128)} %bitcast.27), calls=%async_computation.2 | async-start | bytes 262144 | tf_op jit(solution)/shard_map/all_to_all | solution.py:155
  198.0 7.0 %all-to-all-done.2 = f32[32,8,128]{2,1,0:T(8,128)S(1)} async-done(((f32[32,8,128]{2,1,0:T(8,128)}), f32[32,8,128]{2,1,0:T(8,128)S(1)}, u32[]{:S(2)}, u32[]{:S(2)}) %all-to-all-start.2) | async-done | bytes 131104 | tf_op jit(solution)/shard_map/all_to_all | solution.py:155
  (72 shorter events, 15.1 us)
Async XLA Ops:
  0.0 159.0 %copy-start = (s32[2048,2]{0,1:T(2,128)S(1)}, s32[2048,2]{0,1:T(2,128)}, u32[]{:S(2)}) copy-start(s32[2048,2]{0,1:T(2,128)} %param.8) | copy-start | bytes 49156
  4.1 7.8 %copy-start.5 = (bf16[8,2,256,256]{3,2,1,0:T(8,128)(2,1)S(1)}, bf16[8,2,256,256]{3,2,1,0:T(8,128)(2,1)}, u32[]{:S(2)}) copy-start(bf16[8,2,256,256]{3,2,1,0:T(8,128)(2,1)} %param.5) | copy-start | bytes 6291460
  4.1 69.3 %all-to-all-start = ((bf16[16,2,256,256]{3,2,1,0:T(8,128)(2,1)}), bf16[16,2,256,256]{3,2,1,0:T(8,128)(2,1)}, u32[]{:S(2)}, u32[]{:S(2)}) async-start(bf16[16,2,256,256]{3,2,1,0:T(8,128)(2,1)} %bitcast.64), calls=%async_computation | async-start | bytes 8388608 | tf_op jit(solution)/shard_map/all_to_all | solution.py:135
  11.9 2.5 %copy-start.7 = (s32[4]{0:T(128)S(1)}, s32[4]{0:T(128)}, u32[]{:S(2)}) copy-start(s32[4]{0:T(128)} %param.7) | copy-start | bytes 52
  13.4 6.6 %collective-permute-start.2 = (bf16[8,2,256,256]{3,2,0,1:T(8,128)(2,1)}, bf16[8,2,256,256]{3,2,0,1:T(8,128)(2,1)}, u32[]{:S(2)}, u32[]{:S(2)}) collective-permute-start(bf16[8,2,256,256]{3,2,0,1:T(8,128)(2,1)} %copy.30), channel_id=1, source_target_pairs={{0,1},{1,0},{2,3},{3,2},{4,5},{5,4},{6,7},{7,6},{8,9},{9,8},{10,11... | collective-permute-start | bytes 6291464 | tf_op jit(solution)/shard_map/ppermute | solution.py:16
  20.0 1.9 copy-start.6
  23.5 52.3 %collective-permute-start.6 = (bf16[2,8,32,256]{3,2,1,0:T(8,128)(2,1)S(1)}, bf16[2,8,32,256]{3,2,1,0:T(8,128)(2,1)S(1)}, u32[]{:S(2)}, u32[]{:S(2)}) collective-permute-start(bf16[2,8,32,256]{3,2,1,0:T(8,128)(2,1)S(1)} %fusion.3), channel_id=1, source_target_pairs={{0,14},{2,0},{4,2},{6,4},{8,6},{10,8},{12,10},{14,12},{1,15},{3,1}... | collective-permute-start | bytes 786440 | tf_op jit(solution)/shard_map/ppermute | solution.py:16
  73.4 97.9 %collective-permute-start = (bf16[16,2,256,256]{3,2,1,0:T(8,128)(2,1)}, bf16[16,2,256,256]{3,2,1,0:T(8,128)(2,1)}, u32[]{:S(2)}, u32[]{:S(2)}) collective-permute-start(bf16[16,2,256,256]{3,2,1,0:T(8,128)(2,1)} %all-to-all-done.e_ref), channel_id=1, source_target_pairs={{0,1},{1,0},{2,3},{3,2},{4,5},{5,4},{6,7},{7,6},{8,9},{9,8},{10,11... | collective-permute-start | bytes 12582920 | tf_op jit(solution)/shard_map/ppermute | solution.py:16
  75.9 12.3 %collective-permute-start.3 = (bf16[2,8,32,256]{3,2,1,0:T(8,128)(2,1)S(1)}, bf16[2,8,32,256]{3,2,1,0:T(8,128)(2,1)S(1)}, u32[]{:S(2)}, u32[]{:S(2)}) collective-permute-start(bf16[2,8,32,256]{3,2,1,0:T(8,128)(2,1)S(1)} %get-tuple-element.9), channel_id=1, source_target_pairs={{0,2},{2,4},{4,6},{6,8},{8,10},{10,12},{12,14},{14,0},{1,3},{3,5},... | collective-permute-start | bytes 786440 | tf_op jit(solution)/shard_map/ppermute | solution.py:16
  77.6 10.6 %collective-permute-start.7 = (bf16[2,8,32,256]{3,2,1,0:T(8,128)(2,1)S(1)}, bf16[2,8,32,256]{3,2,1,0:T(8,128)(2,1)S(1)}, u32[]{:S(2)}, u32[]{:S(2)}) collective-permute-start(bf16[2,8,32,256]{3,2,1,0:T(8,128)(2,1)S(1)} %get-tuple-element.10), channel_id=1, source_target_pairs={{0,14},{2,0},{4,2},{6,4},{8,6},{10,8},{12,10},{14,12},{1,15},{3,1}... | collective-permute-start | bytes 786440 | tf_op jit(solution)/shard_map/ppermute | solution.py:16
  88.4 8.6 %collective-permute-start.4 = (bf16[2,8,32,256]{3,2,1,0:T(8,128)(2,1)S(1)}, bf16[2,8,32,256]{3,2,1,0:T(8,128)(2,1)S(1)}, u32[]{:S(2)}, u32[]{:S(2)}) collective-permute-start(bf16[2,8,32,256]{3,2,1,0:T(8,128)(2,1)S(1)} %get-tuple-element.7), channel_id=1, source_target_pairs={{0,2},{2,4},{4,6},{6,8},{8,10},{10,12},{12,14},{14,0},{1,3},{3,5},... | collective-permute-start | bytes 786440 | tf_op jit(solution)/shard_map/ppermute | solution.py:16
  88.5 8.5 %collective-permute-start.8 = (bf16[2,8,32,256]{3,2,1,0:T(8,128)(2,1)S(1)}, bf16[2,8,32,256]{3,2,1,0:T(8,128)(2,1)S(1)}, u32[]{:S(2)}, u32[]{:S(2)}) collective-permute-start(bf16[2,8,32,256]{3,2,1,0:T(8,128)(2,1)S(1)} %get-tuple-element.8), channel_id=1, source_target_pairs={{0,14},{2,0},{4,2},{6,4},{8,6},{10,8},{12,10},{14,12},{1,15},{3,1}... | collective-permute-start | bytes 786440 | tf_op jit(solution)/shard_map/ppermute | solution.py:16
  97.1 6.4 %collective-permute-start.9 = (bf16[2,8,32,256]{3,2,1,0:T(8,128)(2,1)S(1)}, bf16[2,8,32,256]{3,2,1,0:T(8,128)(2,1)S(1)}, u32[]{:S(2)}, u32[]{:S(2)}) collective-permute-start(bf16[2,8,32,256]{3,2,1,0:T(8,128)(2,1)S(1)} %get-tuple-element.6), channel_id=1, source_target_pairs={{0,14},{2,0},{4,2},{6,4},{8,6},{10,8},{12,10},{14,12},{1,15},{3,1}... | collective-permute-start | bytes 786440 | tf_op jit(solution)/shard_map/ppermute | solution.py:16
  99.6 7.0 %collective-permute-start.5 = (bf16[2,8,32,256]{3,2,1,0:T(8,128)(2,1)S(1)}, bf16[2,8,32,256]{3,2,1,0:T(8,128)(2,1)S(1)}, u32[]{:S(2)}, u32[]{:S(2)}) collective-permute-start(bf16[2,8,32,256]{3,2,1,0:T(8,128)(2,1)S(1)} %get-tuple-element.5), channel_id=1, source_target_pairs={{0,2},{2,4},{4,6},{6,8},{8,10},{10,12},{12,14},{14,0},{1,3},{3,5},... | collective-permute-start | bytes 786440 | tf_op jit(solution)/shard_map/ppermute | solution.py:16
  126.7 9.1 %collective-permute-start.11 = (bf16[32,32,256]{2,1,0:T(8,128)(2,1)S(1)}, bf16[32,32,256]{2,1,0:T(8,128)(2,1)S(1)}, u32[]{:S(2)}, u32[]{:S(2)}) collective-permute-start(bf16[32,32,256]{2,1,0:T(8,128)(2,1)S(1)} %bitcast.59), channel_id=1, source_target_pairs={{0,14},{2,0},{4,2},{6,4},{8,6},{10,8},{12,10},{14,12},{1,15},{3,1}... | collective-permute-start | bytes 1572872 | tf_op jit(solution)/shard_map/ppermute | solution.py:16
  127.1 10.5 %collective-permute-start.10 = (bf16[32,32,256]{2,1,0:T(8,128)(2,1)S(1)}, bf16[32,32,256]{2,1,0:T(8,128)(2,1)S(1)}, u32[]{:S(2)}, u32[]{:S(2)}) collective-permute-start(bf16[32,32,256]{2,1,0:T(8,128)(2,1)S(1)} %bitcast.60), channel_id=1, source_target_pairs={{0,2},{2,4},{4,6},{6,8},{8,10},{10,12},{12,14},{14,0},{1,3},{3,5},... | collective-permute-start | bytes 1572872 | tf_op jit(solution)/shard_map/ppermute | solution.py:16
  135.8 10.2 %collective-permute-start.13 = (bf16[32,32,256]{2,1,0:T(8,128)(2,1)S(1)}, bf16[32,32,256]{2,1,0:T(8,128)(2,1)S(1)}, u32[]{:S(2)}, u32[]{:S(2)}) collective-permute-start(bf16[32,32,256]{2,1,0:T(8,128)(2,1)S(1)} %collective-permute-done.11.s_ref), channel_id=1, source_target_pairs={{0,14},{2,0},{4,2},{6,4},{8,6},{10,8},{12,10},{14,12},{1,15},{3,1}... | collective-permute-start | bytes 1572872 | tf_op jit(solution)/shard_map/ppermute | solution.py:16
  137.6 10.4 %collective-permute-start.12 = (bf16[32,32,256]{2,1,0:T(8,128)(2,1)S(1)}, bf16[32,32,256]{2,1,0:T(8,128)(2,1)}, u32[]{:S(2)}, u32[]{:S(2)}) collective-permute-start(bf16[32,32,256]{2,1,0:T(8,128)(2,1)S(1)} %collective-permute-done.10.s_ref), channel_id=1, source_target_pairs={{0,2},{2,4},{4,6},{6,8},{8,10},{10,12},{12,14},{14,0},{1,3},{3,5},... | collective-permute-start | bytes 1572872 | tf_op jit(solution)/shard_map/ppermute | solution.py:16
  137.6 0.9 copy-start.1
  146.1 16.0 %copy-start.3 = (bf16[32,32,256]{2,1,0:T(8,128)(2,1)}, bf16[32,32,256]{2,1,0:T(8,128)(2,1)S(1)}, u32[]{:S(2)}) copy-start(bf16[32,32,256]{2,1,0:T(8,128)(2,1)S(1)} %collective-permute-done.13.s_ref) | copy-start | bytes 1572868
  146.1 13.0 %collective-permute-start.15 = (bf16[32,32,256]{2,1,0:T(8,128)(2,1)S(1)}, bf16[32,32,256]{2,1,0:T(8,128)(2,1)S(1)}, u32[]{:S(2)}, u32[]{:S(2)}) collective-permute-start(bf16[32,32,256]{2,1,0:T(8,128)(2,1)S(1)} %collective-permute-done.13.s_ref), channel_id=1, source_target_pairs={{0,14},{2,0},{4,2},{6,4},{8,6},{10,8},{12,10},{14,12},{1,15},{3,1}... | collective-permute-start | bytes 1572872 | tf_op jit(solution)/shard_map/ppermute | solution.py:16
  148.0 12.8 %collective-permute-start.14 = (bf16[32,32,256]{2,1,0:T(8,128)(2,1)}, bf16[32,32,256]{2,1,0:T(8,128)(2,1)S(1)}, u32[]{:S(2)}, u32[]{:S(2)}) collective-permute-start(bf16[32,32,256]{2,1,0:T(8,128)(2,1)} %collective-permute-done.12.s_ref), channel_id=1, source_target_pairs={{0,2},{2,4},{4,6},{6,8},{8,10},{10,12},{12,14},{14,0},{1,3},{3,5},... | collective-permute-start | bytes 1572872 | tf_op jit(solution)/shard_map/ppermute | solution.py:16
  149.2 13.0 %collective-permute-start.1 = (bf16[2,256,256]{1,2,0:T(8,128)(2,1)S(1)}, bf16[2,256,256]{1,2,0:T(8,128)(2,1)S(1)}, u32[]{:S(2)}, u32[]{:S(2)}) collective-permute-start(bf16[2,256,256]{1,2,0:T(8,128)(2,1)S(1)} %bitcast.71), channel_id=1, source_target_pairs={{0,1},{1,0},{2,3},{3,2},{4,5},{5,4},{6,7},{7,6},{8,9},{9,8},{10,11... | collective-permute-start | bytes 786440 | tf_op jit(solution)/shard_map/ppermute | solution.py:16
  159.8 10.3 %collective-permute-start.17 = (bf16[16,32,256]{2,1,0:T(8,128)(2,1)}, bf16[16,32,256]{2,1,0:T(8,128)(2,1)}, u32[]{:S(2)}, u32[]{:S(2)}) collective-permute-start(bf16[16,32,256]{2,1,0:T(8,128)(2,1)} %slice.17), channel_id=1, source_target_pairs={{0,14},{2,0},{4,2},{6,4},{8,6},{10,8},{12,10},{14,12},{1,15},{3,1}... | collective-permute-start | bytes 786440 | tf_op jit(solution)/shard_map/ppermute | solution.py:16
  161.5 8.6 %collective-permute-start.16 = (bf16[16,32,256]{2,1,0:T(8,128)(2,1)}, bf16[16,32,256]{2,1,0:T(8,128)(2,1)}, u32[]{:S(2)}, u32[]{:S(2)}) collective-permute-start(bf16[16,32,256]{2,1,0:T(8,128)(2,1)} %slice.16), channel_id=1, source_target_pairs={{0,2},{2,4},{4,6},{6,8},{8,10},{10,12},{12,14},{14,0},{1,3},{3,5},... | collective-permute-start | bytes 786440 | tf_op jit(solution)/shard_map/ppermute | solution.py:16
  180.3 1.1 copy-start.4
  183.3 1.1 copy-start.2
  185.6 19.4 %all-to-all-start.2 = ((f32[32,8,128]{2,1,0:T(8,128)}), f32[32,8,128]{2,1,0:T(8,128)S(1)}, u32[]{:S(2)}, u32[]{:S(2)}) async-start(f32[32,8,128]{2,1,0:T(8,128)} %bitcast.27), calls=%async_computation.2 | async-start | bytes 262144 | tf_op jit(solution)/shard_map/all_to_all | solution.py:155

commit v2 on v1

v2 whole, which is shorter than its diff:
```python
import jax
import jax.numpy as jnp
from jax import lax
from jax.experimental import pallas as pl
from jax.experimental.pallas import tpu as pltpu
from jax.experimental.layout import Layout, with_layout_constraint
from jax.sharding import Mesh, PartitionSpec as P

CLASSES = 4
LANES = 128
F32 = jnp.float32
BF16 = jnp.bfloat16


def shift(block, axis, step):
    size = lax.axis_size(axis)
    return lax.ppermute(block, axis, [(i, (i + step) % size) for i in range(size)])


def sandwich_kernel(e_ref, p_ref, w_ref, wide):
    ops, modes = e_ref.shape[:2]
    prop = p_ref[...]
    turned = prop.T
    for a in range(ops):
        half = jnp.dot(e_ref[a], prop, preferred_element_type=F32).astype(BF16)
        whole = jnp.dot(turned, half, preferred_element_type=F32)
        for part in range(modes // LANES):
            wide[part, pl.ds(a, modes, stride=ops), :] = whole[:, part * LANES : (part + 1) * LANES]
    for part in range(modes // LANES):
        w_ref[:, :, part * LANES : (part + 1) * LANES] = wide[part].reshape(modes, ops, LANES).astype(BF16)


def sandwiches(elements, prop):
    ops, modes, _ = elements.shape
    return pl.pallas_call(
        sandwich_kernel,
        out_shape=jax.ShapeDtypeStruct((modes, ops, modes), BF16),
        scratch_shapes=[pltpu.VMEM((modes // LANES, modes * ops, LANES), F32)],
        compiler_params=pltpu.CompilerParams(vmem_limit_bytes=16 * 2**20),
        cost_estimate=pl.CostEstimate(
            flops=4 * ops * modes**3, bytes_accessed=4 * ops * modes**2, transcendentals=0
        ),
    )(elements, prop)


def double_kernel(time, e_ref, o_ref, held, get_sem, put_sem):
    get = pltpu.make_async_copy(e_ref.at[:, time], held, get_sem)
    puts = [pltpu.make_async_copy(held, o_ref.at[:, twin], put_sem.at[twin]) for twin in range(2)]
    get.start()
    get.wait()
    for put in puts:
        put.start()
    for put in puts:
        put.wait()


def doubled(elements, time, limit):
    ops, _, modes, _ = elements.shape
    out = pl.pallas_call(
        lambda *refs: double_kernel(time, *refs),
        in_specs=[pl.BlockSpec(memory_space=pl.ANY)],
        out_specs=pl.BlockSpec(memory_space=pl.ANY),
        out_shape=jax.ShapeDtypeStruct((ops, 2, modes, modes), BF16),
        scratch_shapes=[
            pltpu.VMEM((ops, modes, modes), BF16),
            pltpu.SemaphoreType.DMA(()),
            pltpu.SemaphoreType.DMA((2,)),
        ],
        compiler_params=pltpu.CompilerParams(vmem_limit_bytes=limit * 2**20),
        cost_estimate=pl.CostEstimate(flops=2**32, bytes_accessed=6 * ops * modes**2, transcendentals=0),
    )(elements)
    return out.reshape(2 * ops, modes, modes)


def slot_kernel(when_ref, own_ref, other_ref, o_ref, zeros, sem):
    z, core = lax.axis_index("z"), lax.axis_index("c")
    times, count = own_ref.shape[1], o_ref.shape[0]
    zeros[...] = jnp.zeros_like(zeros)
    for slot in range(count):
        when = when_ref[2 * slot + core]
        holder, inside = when // times, when % times
        here = holder // 2 == z
        mine = here & (holder % 2 == core)

        def fetch(source, slot=slot):
            pltpu.make_async_copy(source, o_ref.at[slot], sem.at[slot]).start()

        pl.when(mine)(lambda inside=inside, fetch=fetch: fetch(own_ref.at[:, inside]))
        pl.when(here & ~mine)(lambda inside=inside, fetch=fetch: fetch(other_ref.at[:, inside]))
        pl.when(~here)(lambda fetch=fetch: fetch(zeros))
    for slot in range(count):
        pltpu.make_async_copy(zeros, o_ref.at[slot], sem.at[slot]).wait()


def slots_of(src_times, own, other):
    ops, _, modes, _ = own.shape
    count = src_times.shape[0] // 2
    return pl.pallas_call(
        slot_kernel,
        in_specs=[pl.BlockSpec(memory_space=pltpu.SMEM)] + [pl.BlockSpec(memory_space=pl.ANY)] * 2,
        out_specs=pl.BlockSpec(memory_space=pltpu.VMEM),
        out_shape=jax.ShapeDtypeStruct((count, ops, modes, modes), BF16),
        scratch_shapes=[pltpu.VMEM((ops, modes, modes), BF16), pltpu.SemaphoreType.DMA((count,))],
        compiler_params=pltpu.CompilerParams(vmem_limit_bytes=8 * 2**20),
    )(src_times, own, other)


def product_kernel(tasks, at_ref, *refs):
    lefts, blocks, outs = refs[: 2 * len(tasks)], refs[2 * len(tasks) : -len(tasks)], refs[-len(tasks) :]
    rows = blocks[0].shape[0]
    for task, numbers in enumerate(tasks):
        total = None
        for number in numbers:
            sources = jnp.concatenate([blocks[number][r] for r in range(rows)], 1)
            base = at_ref[number] * rows
            pair = lefts[2 * task : 2 * task + 2]
            left = jnp.concatenate([jnp.concatenate([w[base + r] for w in pair], 0) for r in range(rows)], 1)
            part = lax.dot_general(left, sources, (((1,), (1,)), ((), ())), preferred_element_type=F32)
            total = part if total is None else total + part
        outs[task][...] = total


def block_products(tasks, found):
    rows, count, modes = found[0][1].shape
    left = tasks[0][0][0].shape[1]
    work = sum(len(numbers) for _, numbers in tasks)
    return pl.pallas_call(
        lambda *refs: product_kernel([numbers for _, numbers in tasks], *refs),
        in_specs=[pl.BlockSpec(memory_space=pltpu.SMEM)]
        + [pl.BlockSpec(memory_space=pltpu.VMEM)] * (2 * len(tasks) + len(found)),
        out_shape=[jax.ShapeDtypeStruct((2 * left, count), F32)] * len(tasks),
        compiler_params=pltpu.CompilerParams(vmem_limit_bytes=8 * 2**20),
        cost_estimate=pl.CostEstimate(
            flops=4 * work * rows * left * count * modes,
            bytes_accessed=2 * work * rows * modes * (2 * left + count),
            transcendentals=0,
        ),
    )(
        jnp.stack([at for at, _ in found]).astype(jnp.int32),
        *[w for pair, _ in tasks for w in pair],
        *[block for _, block in found],
    )


def per_device(elementals, perambulators, src_times, pair_ops, conj_flags):
    ops, times, modes, _ = elementals.shape
    sources = perambulators.shape[1]
    z, core = lax.axis_index("z"), lax.axis_index("c")
    planes = lax.axis_size("z")
    chips = lax.axis_size("x") * lax.axis_size("y")
    place = lax.axis_index("x") * lax.axis_size("y") + lax.axis_index("y")
    k_half = place % 2
    my_k = 2 * k_half + core
    xy = ("x", "y")

    tie = lambda *values: lax.optimization_barrier(values)
    props_near = lax.dynamic_index_in_dim(perambulators, my_k, 1, keepdims=False)
    props_far = lax.dynamic_index_in_dim(perambulators, 2 * k_half + 1 - core, 1, keepdims=False)

    double = doubled(elementals, 0, 60)

    beside = shift(elementals, "c", 1)
    beside, double = tie(beside, double)
    slots = slots_of(src_times, elementals, beside)

    rows, reach = modes // planes, planes // 2
    chunk = lambda j: lax.dynamic_slice_in_dim(slots, j % planes * rows, rows, 2)
    down = shift(chunk(z + planes - reach), "z", -1)
    first = lax.all_to_all(double, xy, 0, 0, tiled=True)
    up = None
    for step in range(1, reach):
        send_down = chunk(z + planes - reach + step) + down
        send_up = chunk(z + reach - step)
        if up is not None:
            send_up = send_up + up
        send_down, send_up = tie(send_down, send_up)
        down, up = shift(send_down, "z", -1), shift(send_up, "z", 1)
        down, up = tie(down, up)
    mine = chunk(z) + up + down
    props_far = shift(props_far, "c", 1)
    first, mine, props_near, props_far = tie(first, mine, props_near, props_far)

    mine = mine.reshape(2, 2, CLASSES, rows, modes).transpose(2, 0, 1, 3, 4)
    mine = jnp.broadcast_to(mine[None], (2,) + mine.shape).reshape(chips, 2 * rows, modes)
    elements, mine = tie(elementals, mine)
    second = lax.all_to_all(doubled(elements, 1, 8), xy, 0, 0, tiled=True)
    mine = lax.all_to_all(mine, xy, 0, 0, tiled=True)
    mine = mine.reshape(2 * chips, rows, modes).transpose(1, 0, 2)

    first_far = shift(first, "c", 1)
    number = lambda offset: (z + planes + offset) % planes
    found = [(number(0), mine)]
    up, down = shift(mine, "z", 1), shift(mine, "z", -1)
    w_near = sandwiches(first, props_near[0])
    up, down, w_near, first_far = tie(up, down, w_near, first_far)
    found += [(number(-1), up), (number(1), down)]
    up, down = shift(up, "z", 1), shift(down, "z", -1)
    w_far = sandwiches(first_far, props_far[0])
    up, down, w_far = tie(up, down, w_far)
    found += [(number(-2), up), (number(2), down)]
    w_first = w_near, w_far
    up, down = shift(up, "z", 1), shift(down, "z", -1)
    (early,) = block_products([(w_first, range(5))], found)
    second, up, down, early = tie(second, up, down, early)
    found += [(number(-3), up), (number(3), down)]
    last = shift(up, "z", 1)
    second_far = shift(second, "c", 1)
    w_second = sandwiches(second, props_near[1]), sandwiches(second_far, props_far[1])
    middle, total = block_products([(w_first, range(5, 7)), (w_second, range(7))], found)
    last, middle = tie(last, middle)
    late = block_products([(w_first, [0]), (w_second, [0])], [(number(reach), last)])
    early, total = early + middle + late[0], total + late[1]
    total = jnp.stack([early.reshape(2, -1), total.reshape(2, -1)], 1)
    by_core = jnp.where(core == 0, total, total[::-1])
    by_core = by_core.reshape(2, 8, -1)
    out = jnp.broadcast_to(by_core[None], (chips,) + by_core.shape).reshape((2 * chips,) + by_core.shape[1:])
    out = lax.all_to_all(out, ("x", "y", "c"), 0, 0, tiled=True)
    groups = 2 * chips
    table = out.reshape(2, CLASSES, 2, 2, times, chips, groups).transpose(5, 0, 1, 4, 2, 3, 6)
    table = table.reshape(CLASSES * groups, times * sources * groups)

    pairs = pair_ops.shape[0] // chips
    local = lax.dynamic_slice_in_dim(pair_ops, place * pairs, pairs, 0)
    flags = lax.dynamic_slice_in_dim(conj_flags, place * pairs, pairs, 0)
    left, right = local[:, 0], local[:, 1]

    def picked(first, second):
        row = (first[:, None] == jnp.arange(CLASSES * groups)[None]).astype(F32)
        lines = jnp.dot(row, table, precision=lax.Precision.HIGHEST, preferred_element_type=F32)
        lines = lines.reshape(pairs, times * sources, groups)
        column = (second // CLASSES)[:, None, None] == jnp.arange(groups)[None, None]
        return jnp.sum(jnp.where(column, lines, 0.0), 2)

    forward, backward = picked(left, right), picked(right, left)
    symmetric = jnp.where(flags[:, None] == 1, 0.5 * (forward + backward), forward)
    return (symmetric / modes).reshape(pairs, times, sources)


def solution(mesh):
    chips = Mesh(mesh.devices.reshape(4, 4, 8, 2), ("x", "y", "z", "c"))
    op, tm = ("x", "y"), ("z", "c")
    return jax.shard_map(
        per_device,
        mesh=chips,
        in_specs=(P(op, tm, None, None), P(tm, None, None, None), P(), P(), P()),
        out_specs=P(op, tm, None),
        check_vma=False,
    )
```

time: 208 us -> 151 us (0.73)
  waiting for transfers between devices: 85.8 us -> 47.9 us
  blocking collectives: 18.6 us -> 0 us
  Pallas kernels: 20 us -> 27.9 us
  between operations: 5.41 us -> 0.46 us
  other arithmetic: 6.16 us -> 3.02 us
    all_to_all x1 -> x3, waiting for transfers between devices: 44.3 us -> 10.9 us  [the longest x1 8.48 us: per_device(): mine = lax.all_to_all(mine, xy, 0, 0, tiled=True)]
    all_to_all x1 -> x0, blocking collectives: 18.6 us -> none  [per_device(): mine = lax.all_to_all(mine, xy, 0, 0, tiled=True)]
    all_to_all x1 -> x3, starting transfers between devices: 7.77 us -> 16.3 us  [the longest x1 6.81 us: per_device(): first = lax.all_to_all(double, xy, 0, 0, tiled=True)]
    pallas_call x10, Pallas kernels: 20 us -> 27.9 us  [the longest x4 17.8 us: sandwiches(): pl.pallas_call(sandwich_kernel, out_shape=jax.ShapeDtypeStruct((modes, op...]
    unnamed x17 -> x30, local copies, waits for them, and re-layouts: 4.06 us -> 9.86 us
    ppermute x18, waiting for transfers between devices: 34.5 us -> 30 us  [shift(): lax.ppermute(block, axis, [(i, (i + step) % size) for i in range(size)])]
    broadcast_in_dim x1 -> x0, local copies, waits for them, and re-layouts: 4.09 us -> none  [per_device(): jnp.broadcast_to(elementals[:, None], (ops, 2, times, modes, modes))]
    all_to_all x1, starting transfers between devices: 11.6 us -> 7.52 us  [per_device(): out = lax.all_to_all(out, ('x', 'y', 'c'), 0, 0, tiled=True)]
  transfers between devices with their start and end apart: 20 -> 22, of which waited for: 8 -> 13; matrix products, arithmetic and copies ran while one was open for 6% -> 3% of each run, Pallas kernels for 4% -> 17%
where the time goes in v2:
time: 151 us
  starting transfers between devices  56.3 us (37%)
  waiting for transfers between devices  47.9 us (32%)
  Pallas kernels  27.9 us (18%)
  local copies, waits for them, and re-layouts  14.4 us (10%)
  other arithmetic  3.02 us (2%)
    ppermute x18, starting transfers between devices, shift(): lax.ppermute(block, axis, [(i, (i + step) % size) for i in range(size)])  32.4 us
    ppermute x18, waiting for transfers between devices, shift(): lax.ppermute(block, axis, [(i, (i + step) % size) for i in range(size)])  30 us
    pallas_call x4, Pallas kernels, sandwiches(): pl.pallas_call(sandwich_kernel, out_shape=jax.ShapeDtypeStruct((modes, op...  17.8 us
    unnamed x30, local copies, waits for them, and re-layouts  9.86 us
    all_to_all x1, waiting for transfers between devices, per_device(): mine = lax.all_to_all(mine, xy, 0, 0, tiled=True)  8.48 us
    all_to_all x1, starting transfers between devices, per_device(): out = lax.all_to_all(out, ('x', 'y', 'c'), 0, 0, tiled=True)  7.52 us
    all_to_all x1, waiting for transfers between devices, per_device(): out = lax.all_to_all(out, ('x', 'y', 'c'), 0, 0, tiled=True)  6.92 us
    all_to_all x1, starting transfers between devices, per_device(): first = lax.all_to_all(double, xy, 0, 0, tiled=True)  6.81 us
  transfers between devices with their start and end apart: 22, of which 13 were waited for; matrix products, arithmetic and copies ran while one was open for 3% of the time, Pallas kernels for 17%

profile of v2, /device:TPU:1, one launch (start us, length us, event | category | flops | bytes accessed | tf_op | source)
XLA Modules:
  0.0 150.5 jit_solution(3046883174066447854)
XLA Ops:
  0.0 3.2 %collective-permute-start = (bf16[8,2,256,256]{3,2,1,0:T(8,128)(2,1)}, bf16[8,2,256,256]{3,2,1,0:T(8,128)(2,1)S(1)}, u32[]{:S(2)}, u32[]{:S(2)}) collective-permute-start(bf16[8,2,256,256]{3,2,1,0:T(8,128)(2,1)} %refs_0_.2), channel_id=1, source_target_pairs={{0,1},{1,0},{2,3},{3,2},{4,5},{5,4},{6,7},{7,6},{8,9},{9,8},{10,11... | collective-permute-start | bytes 6291464 | tf_op jit(solution)/shard_map/ppermute | solution.py:17
  3.2 2.7 %shard_map.55 = bf16[8,2,256,256]{3,2,1,0:T(8,128)(2,1)} custom-call(bf16[8,2,256,256]{3,2,1,0:T(8,128)(2,1)} %refs_0_.2), custom_call_target="tpu_custom_call" | custom-call | flops 4294967296 | bytes 3145728 | tf_op jit(solution)/shard_map/pallas_call | solution.py:59
  8.6 1.6 %copy-done.4 = bf16[8,2,256,256]{3,2,1,0:T(8,128)(2,1)S(1)} copy-done((bf16[8,2,256,256]{3,2,1,0:T(8,128)(2,1)S(1)}, bf16[8,2,256,256]{3,2,1,0:T(8,128)(2,1)}, u32[]{:S(2)}) %copy-start.4) | copy-done | bytes 2097176
  12.6 3.9 %collective-permute-start.1 = (bf16[2,8,32,256]{3,2,1,0:T(8,128)(2,1)S(1)}, bf16[2,8,32,256]{3,2,1,0:T(8,128)(2,1)S(1)}, u32[]{:S(2)}, u32[]{:S(2)}) collective-permute-start(bf16[2,8,32,256]{3,2,1,0:T(8,128)(2,1)S(1)} %get-tuple-element.84), channel_id=1, source_target_pairs={{0,14},{2,0},{4,2},{6,4},{8,6},{10,8},{12,10},{14,12},{1,15},{3,1}... | collective-permute-start | bytes 786440 | tf_op jit(solution)/shard_map/ppermute | solution.py:17
  16.5 6.8 %all-to-all-start = ((bf16[16,256,256]{2,1,0:T(8,128)(2,1)}), bf16[16,256,256]{2,1,0:T(8,128)(2,1)}, u32[]{:S(2)}, u32[]{:S(2)}) async-start(bf16[16,256,256]{2,1,0:T(8,128)(2,1)} %bitcast.58), calls=%async_computation | async-start | bytes 4194304 | tf_op jit(solution)/shard_map/all_to_all | solution.py:169
  23.5 2.0 %collective-permute-start.2 = (bf16[2,8,32,256]{3,2,1,0:T(8,128)(2,1)S(1)}, bf16[2,8,32,256]{3,2,1,0:T(8,128)(2,1)S(1)}, u32[]{:S(2)}, u32[]{:S(2)}) collective-permute-start(bf16[2,8,32,256]{3,2,1,0:T(8,128)(2,1)S(1)} %dynamic-slice_add_fusion.2), channel_id=1, source_target_pairs={{0,14},{2,0},{4,2},{6,4},{8,6},{10,8},{12,10},{14,12},{1,15},{3,1}... | collective-permute-start | bytes 786440 | tf_op jit(solution)/shard_map/ppermute | solution.py:17
  25.4 5.1 %collective-permute-done.2 = bf16[2,8,32,256]{3,2,1,0:T(8,128)(2,1)S(1)} collective-permute-done((bf16[2,8,32,256]{3,2,1,0:T(8,128)(2,1)S(1)}, bf16[2,8,32,256]{3,2,1,0:T(8,128)(2,1)S(1)}, u32[]{:S(2)}, u32[]{:S(2)}) %collective-permute-start.2) | collective-permute-done | bytes 262176 | tf_op jit(solution)/shard_map/ppermute | solution.py:17
  30.5 2.5 %collective-permute-done.3 = bf16[2,8,32,256]{3,2,1,0:T(8,128)(2,1)S(1)} collective-permute-done((bf16[2,8,32,256]{3,2,1,0:T(8,128)(2,1)S(1)}, bf16[2,8,32,256]{3,2,1,0:T(8,128)(2,1)S(1)}, u32[]{:S(2)}, u32[]{:S(2)}) %collective-permute-start.3) | collective-permute-done | bytes 262176 | tf_op jit(solution)/shard_map/ppermute | solution.py:17
  34.8 4.2 %collective-permute-done.4 = bf16[2,8,32,256]{3,2,1,0:T(8,128)(2,1)S(1)} collective-permute-done((bf16[2,8,32,256]{3,2,1,0:T(8,128)(2,1)S(1)}, bf16[2,8,32,256]{3,2,1,0:T(8,128)(2,1)S(1)}, u32[]{:S(2)}, u32[]{:S(2)}) %collective-permute-start.4) | collective-permute-done | bytes 262176 | tf_op jit(solution)/shard_map/ppermute | solution.py:17
  43.3 3.7 %collective-permute-start.8 = (bf16[2,256,256]{2,1,0:T(8,128)(2,1)S(1)}, bf16[2,256,256]{2,1,0:T(8,128)(2,1)S(1)}, u32[]{:S(2)}, u32[]{:S(2)}) collective-permute-start(bf16[2,256,256]{2,1,0:T(8,128)(2,1)S(1)} %get-tuple-element.85), channel_id=1, source_target_pairs={{0,1},{1,0},{2,3},{3,2},{4,5},{5,4},{6,7},{7,6},{8,9},{9,8},{10,11... | collective-permute-start | bytes 786440 | tf_op jit(solution)/shard_map/ppermute | solution.py:17
  49.0 2.4 %all-to-all-done.e_ref = bf16[16,256,256]{2,1,0:T(8,128)(2,1)} async-done(((bf16[16,256,256]{2,1,0:T(8,128)(2,1)}), bf16[16,256,256]{2,1,0:T(8,128)(2,1)}, u32[]{:S(2)}, u32[]{:S(2)}) %all-to-all-start) | async-done | bytes 2097184 | tf_op jit(solution)/shard_map/all_to_all | solution.py:169
  51.4 3.3 %collective-permute-start.11 = (bf16[16,256,256]{2,1,0:T(8,128)(2,1)}, bf16[16,256,256]{2,1,0:T(8,128)(2,1)}, u32[]{:S(2)}, u32[]{:S(2)}) collective-permute-start(bf16[16,256,256]{2,1,0:T(8,128)(2,1)} %all-to-all-done.e_ref), channel_id=1, source_target_pairs={{0,1},{1,0},{2,3},{3,2},{4,5},{5,4},{6,7},{7,6},{8,9},{9,8},{10,11... | collective-permute-start | bytes 6291464 | tf_op jit(solution)/shard_map/ppermute | solution.py:17
  55.6 5.1 %all-to-all-start.2 = ((bf16[16,64,256]{2,1,0:T(8,128)(2,1)}), bf16[16,64,256]{2,1,0:T(8,128)(2,1)S(1)}, u32[]{:S(2)}, u32[]{:S(2)}) async-start(bf16[16,64,256]{2,1,0:T(8,128)(2,1)} %bitcast.8), calls=%async_computation.2 | async-start | bytes 1048576 | tf_op jit(solution)/shard_map/all_to_all | solution.py:187
  62.4 8.5 %all-to-all-done.2 = bf16[16,64,256]{2,1,0:T(8,128)(2,1)S(1)} async-done(((bf16[16,64,256]{2,1,0:T(8,128)(2,1)}), bf16[16,64,256]{2,1,0:T(8,128)(2,1)S(1)}, u32[]{:S(2)}, u32[]{:S(2)}) %all-to-all-start.2) | async-done | bytes 524320 | tf_op jit(solution)/shard_map/all_to_all | solution.py:187
  70.9 4.4 %all-to-all-start.1 = ((bf16[16,256,256]{2,1,0:T(8,128)(2,1)}), bf16[16,256,256]{2,1,0:T(8,128)(2,1)}, u32[]{:S(2)}, u32[]{:S(2)}) async-start(bf16[16,256,256]{2,1,0:T(8,128)(2,1)} %bitcast.56), calls=%async_computation.1 | async-start | bytes 4194304 | tf_op jit(solution)/shard_map/all_to_all | solution.py:186
  75.9 2.4 %collective-permute-start.10 = (bf16[32,32,256]{2,1,0:T(8,128)(2,1)S(1)}, bf16[32,32,256]{2,1,0:T(8,128)(2,1)S(1)}, u32[]{:S(2)}, u32[]{:S(2)}) collective-permute-start(bf16[32,32,256]{2,1,0:T(8,128)(2,1)S(1)} %bitcast.53), channel_id=1, source_target_pairs={{0,14},{2,0},{4,2},{6,4},{8,6},{10,8},{12,10},{14,12},{1,15},{3,1}... | collective-permute-start | bytes 1572872 | tf_op jit(solution)/shard_map/ppermute | solution.py:17
  78.4 4.4 %shard_map.58.refs_1_ = bf16[256,16,256]{2,1,0:T(8,128)(2,1)S(1)} custom-call(bf16[16,256,256]{2,1,0:T(8,128)(2,1)} %all-to-all-done.e_ref, bf16[256,256]{1,0:T(8,128)(2,1)S(1)} %get-tuple-element.90.p_ref), custom_call_target="tpu_custom_call" | custom-call | flops 1073741824 | bytes 4194304 | tf_op jit(solution)/shard_map/pallas_call | solution.py:35
  82.8 5.3 %collective-permute-done.9.refs_4_.refs_6_ = bf16[32,32,256]{2,1,0:T(8,128)(2,1)S(1)} collective-permute-done((bf16[32,32,256]{2,1,0:T(8,128)(2,1)S(1)}, bf16[32,32,256]{2,1,0:T(8,128)(2,1)S(1)}, u32[]{:S(2)}, u32[]{:S(2)}) %collective-permute-start.9) | collective-permute-done | bytes 524320 | tf_op jit(solution)/shard_map/ppermute | solution.py:17
  88.2 2.7 %collective-permute-start.13 = (bf16[32,32,256]{2,1,0:T(8,128)(2,1)S(1)}, bf16[32,32,256]{2,1,0:T(8,128)(2,1)}, u32[]{:S(2)}, u32[]{:S(2)}) collective-permute-start(bf16[32,32,256]{2,1,0:T(8,128)(2,1)S(1)} %collective-permute-done.10.refs_5_.refs_7_), channel_id=1, source_target_pairs={{0,14},{2,0},{4,2},{6,4},{8,6},{10,8},{12,10},{14,12},{1,15},{3,1}... | collective-permute-start | bytes 1572872 | tf_op jit(solution)/shard_map/ppermute | solution.py:17
  90.9 4.4 %shard_map.59.refs_2_ = bf16[256,16,256]{2,1,0:T(8,128)(2,1)S(1)} custom-call(bf16[16,256,256]{2,1,0:T(8,128)(2,1)} %collective-permute-done.11.e_ref, bf16[256,256]{1,0:T(8,128)(2,1)S(1)} %get-tuple-element.88.p_ref), custom_call_target="tpu_custom_call" | custom-call | flops 1073741824 | bytes 4194304 | tf_op jit(solution)/shard_map/pallas_call | solution.py:35
  96.6 3.2 %collective-permute-done.12.refs_6_.refs_8_ = bf16[32,32,256]{2,1,0:T(8,128)(2,1)} collective-permute-done((bf16[32,32,256]{2,1,0:T(8,128)(2,1)S(1)}, bf16[32,32,256]{2,1,0:T(8,128)(2,1)}, u32[]{:S(2)}, u32[]{:S(2)}) %collective-permute-start.12) | collective-permute-done | bytes 524320 | tf_op jit(solution)/shard_map/ppermute | solution.py:17
  99.8 2.7 %collective-permute-start.15 = (bf16[32,32,256]{2,1,0:T(8,128)(2,1)}, bf16[32,32,256]{2,1,0:T(8,128)(2,1)}, u32[]{:S(2)}, u32[]{:S(2)}) collective-permute-start(bf16[32,32,256]{2,1,0:T(8,128)(2,1)} %collective-permute-done.13.refs_7_.refs_9_), channel_id=1, source_target_pairs={{0,14},{2,0},{4,2},{6,4},{8,6},{10,8},{12,10},{14,12},{1,15},{3,1}... | collective-permute-start | bytes 1572872 | tf_op jit(solution)/shard_map/ppermute | solution.py:17
  102.6 1.6 %copy-done.2 = bf16[256,16,256]{2,1,0:T(8,128)(2,1)S(1)} copy-done((bf16[256,16,256]{2,1,0:T(8,128)(2,1)S(1)}, bf16[256,16,256]{2,1,0:T(8,128)(2,1)}, u32[]{:S(2)}) %copy-start.2) | copy-done | bytes 2097176
  105.2 2.0 %shard_map.60 = f32[32,32]{1,0:T(8,128)S(1)} custom-call(s32[5]{0:T(128)S(1)} %stack.43.refs_0_, bf16[256,16,256]{2,1,0:T(8,128)(2,1)S(1)} %shard_map.58.refs_1_, bf16[256,16,256]{2,1,0:T(8,128)(2,1)S(1)} %copy-done.2, bf16[32,32,256]{2,1,0:T(8,128)(2,1)S(1)} %bitcast.54, bf16[32,32,256]{2,1,0:T(8,128)(2,1)S(1)} %collective-permute-done.9.refs_4_.refs_6_, ...), custom_call_target="tpu_custom_call" | custom-call | flops 83886080 | bytes 5242880 | tf_op jit(solution)/shard_map/pallas_call | solution.py:127
  107.2 3.5 %collective-permute-done.14.refs_10_ = bf16[32,32,256]{2,1,0:T(8,128)(2,1)} collective-permute-done((bf16[32,32,256]{2,1,0:T(8,128)(2,1)}, bf16[32,32,256]{2,1,0:T(8,128)(2,1)}, u32[]{:S(2)}, u32[]{:S(2)}) %collective-permute-start.14) | collective-permute-done | bytes 524320 | tf_op jit(solution)/shard_map/ppermute | solution.py:17
  110.7 5.0 %collective-permute-start.17 = (bf16[16,256,256]{2,1,0:T(8,128)(2,1)}, bf16[16,256,256]{2,1,0:T(8,128)(2,1)}, u32[]{:S(2)}, u32[]{:S(2)}) collective-permute-start(bf16[16,256,256]{2,1,0:T(8,128)(2,1)} %all-to-all-done.1.e_ref), channel_id=1, source_target_pairs={{0,1},{1,0},{2,3},{3,2},{4,5},{5,4},{6,7},{7,6},{8,9},{9,8},{10,11... | collective-permute-start | bytes 6291464 | tf_op jit(solution)/shard_map/ppermute | solution.py:17
  115.8 4.4 %shard_map.61.refs_3_ = bf16[256,16,256]{2,1,0:T(8,128)(2,1)S(1)} custom-call(bf16[16,256,256]{2,1,0:T(8,128)(2,1)} %all-to-all-done.1.e_ref, bf16[256,256]{1,0:T(8,128)(2,1)S(1)} %get-tuple-element.89.p_ref), custom_call_target="tpu_custom_call" | custom-call | flops 1073741824 | bytes 4194304 | tf_op jit(solution)/shard_map/pallas_call | solution.py:35
  120.3 4.5 %shard_map.62.refs_4_ = bf16[256,16,256]{2,1,0:T(8,128)(2,1)S(1)} custom-call(bf16[16,256,256]{2,1,0:T(8,128)(2,1)} %collective-permute-done.17.e_ref, bf16[256,256]{1,0:T(8,128)(2,1)S(1)} %get-tuple-element.87.p_ref), custom_call_target="tpu_custom_call" | custom-call | flops 1073741824 | bytes 4194304 | tf_op jit(solution)/shard_map/pallas_call | solution.py:35
  124.8 2.9 %shard_map.63 = (f32[32,32]{1,0:T(8,128)S(1)}, f32[32,32]{1,0:T(8,128)S(1)}) custom-call(s32[7]{0:T(128)S(1)} %stack.46.refs_0_, bf16[256,16,256]{2,1,0:T(8,128)(2,1)S(1)} %shard_map.58.refs_1_, bf16[256,16,256]{2,1,0:T(8,128)(2,1)S(1)} %copy-done.3, bf16[256,16,256]{2,1,0:T(8,128)(2,1)S(1)} %shard_map.61.refs_3_, ...), custom_call_target="tpu_custom_call" | custom-call | flops 150994944 | bytes 9437184 | tf_op jit(solution)/shard_map/pallas_call | solution.py:127
  127.7 2.7 %collective-permute-done.16.refs_5_ = bf16[32,32,256]{2,1,0:T(8,128)(2,1)} collective-permute-done((bf16[32,32,256]{2,1,0:T(8,128)(2,1)}, bf16[32,32,256]{2,1,0:T(8,128)(2,1)}, u32[]{:S(2)}, u32[]{:S(2)}) %collective-permute-start.16) | collective-permute-done | bytes 524320 | tf_op jit(solution)/shard_map/ppermute | solution.py:17
  132.8 7.5 %all-to-all-start.3 = ((f32[32,8,128]{2,1,0:T(8,128)}), f32[32,8,128]{2,1,0:T(8,128)S(1)}, u32[]{:S(2)}, u32[]{:S(2)}) async-start(f32[32,8,128]{2,1,0:T(8,128)} %bitcast.24), calls=%async_computation.3 | async-start | bytes 262144 | tf_op jit(solution)/shard_map/all_to_all | solution.py:217
  141.1 6.9 %all-to-all-done.3 = f32[32,8,128]{2,1,0:T(8,128)S(1)} async-done(((f32[32,8,128]{2,1,0:T(8,128)}), f32[32,8,128]{2,1,0:T(8,128)S(1)}, u32[]{:S(2)}, u32[]{:S(2)}) %all-to-all-start.3) | async-done | bytes 131104 | tf_op jit(solution)/shard_map/all_to_all | solution.py:217
  (85 shorter events, 24.6 us)
Async XLA Ops:
  0.0 115.7 %copy-start = (s32[2048,2]{0,1:T(2,128)S(1)}, s32[2048,2]{0,1:T(2,128)}, u32[]{:S(2)}) copy-start(s32[2048,2]{0,1:T(2,128)} %param.8) | copy-start | bytes 49156
  0.0 7.2 %collective-permute-start = (bf16[8,2,256,256]{3,2,1,0:T(8,128)(2,1)}, bf16[8,2,256,256]{3,2,1,0:T(8,128)(2,1)S(1)}, u32[]{:S(2)}, u32[]{:S(2)}) collective-permute-start(bf16[8,2,256,256]{3,2,1,0:T(8,128)(2,1)} %refs_0_.2), channel_id=1, source_target_pairs={{0,1},{1,0},{2,3},{3,2},{4,5},{5,4},{6,7},{7,6},{8,9},{9,8},{10,11... | collective-permute-start | bytes 6291464 | tf_op jit(solution)/shard_map/ppermute | solution.py:17
  3.2 5.3 %copy-start.12 = (s32[4]{0:T(128)S(1)}, s32[4]{0:T(128)}, u32[]{:S(2)}) copy-start(s32[4]{0:T(128)} %when_ref.1) | copy-start | bytes 52
  8.6 1.6 %copy-start.4 = (bf16[8,2,256,256]{3,2,1,0:T(8,128)(2,1)S(1)}, bf16[8,2,256,256]{3,2,1,0:T(8,128)(2,1)}, u32[]{:S(2)}) copy-start(bf16[8,2,256,256]{3,2,1,0:T(8,128)(2,1)} %refs_0_.2) | copy-start | bytes 6291460
  12.6 10.8 %collective-permute-start.1 = (bf16[2,8,32,256]{3,2,1,0:T(8,128)(2,1)S(1)}, bf16[2,8,32,256]{3,2,1,0:T(8,128)(2,1)S(1)}, u32[]{:S(2)}, u32[]{:S(2)}) collective-permute-start(bf16[2,8,32,256]{3,2,1,0:T(8,128)(2,1)S(1)} %get-tuple-element.84), channel_id=1, source_target_pairs={{0,14},{2,0},{4,2},{6,4},{8,6},{10,8},{12,10},{14,12},{1,15},{3,1}... | collective-permute-start | bytes 786440 | tf_op jit(solution)/shard_map/ppermute | solution.py:17
  16.5 34.9 %all-to-all-start = ((bf16[16,256,256]{2,1,0:T(8,128)(2,1)}), bf16[16,256,256]{2,1,0:T(8,128)(2,1)}, u32[]{:S(2)}, u32[]{:S(2)}) async-start(bf16[16,256,256]{2,1,0:T(8,128)(2,1)} %bitcast.58), calls=%async_computation | async-start | bytes 4194304 | tf_op jit(solution)/shard_map/all_to_all | solution.py:169
  23.5 7.1 %collective-permute-start.2 = (bf16[2,8,32,256]{3,2,1,0:T(8,128)(2,1)S(1)}, bf16[2,8,32,256]{3,2,1,0:T(8,128)(2,1)S(1)}, u32[]{:S(2)}, u32[]{:S(2)}) collective-permute-start(bf16[2,8,32,256]{3,2,1,0:T(8,128)(2,1)S(1)} %dynamic-slice_add_fusion.2), channel_id=1, source_target_pairs={{0,14},{2,0},{4,2},{6,4},{8,6},{10,8},{12,10},{14,12},{1,15},{3,1}... | collective-permute-start | bytes 786440 | tf_op jit(solution)/shard_map/ppermute | solution.py:17
  25.4 7.6 %collective-permute-start.3 = (bf16[2,8,32,256]{3,2,1,0:T(8,128)(2,1)S(1)}, bf16[2,8,32,256]{3,2,1,0:T(8,128)(2,1)S(1)}, u32[]{:S(2)}, u32[]{:S(2)}) collective-permute-start(bf16[2,8,32,256]{3,2,1,0:T(8,128)(2,1)S(1)} %get-tuple-element.45), channel_id=1, source_target_pairs={{0,2},{2,4},{4,6},{6,8},{8,10},{10,12},{12,14},{14,0},{1,3},{3,5},... | collective-permute-start | bytes 786440 | tf_op jit(solution)/shard_map/ppermute | solution.py:17
  33.3 5.7 %collective-permute-start.4 = (bf16[2,8,32,256]{3,2,1,0:T(8,128)(2,1)S(1)}, bf16[2,8,32,256]{3,2,1,0:T(8,128)(2,1)S(1)}, u32[]{:S(2)}, u32[]{:S(2)}) collective-permute-start(bf16[2,8,32,256]{3,2,1,0:T(8,128)(2,1)S(1)} %get-tuple-element.48), channel_id=1, source_target_pairs={{0,14},{2,0},{4,2},{6,4},{8,6},{10,8},{12,10},{14,12},{1,15},{3,1}... | collective-permute-start | bytes 786440 | tf_op jit(solution)/shard_map/ppermute | solution.py:17
  33.6 6.8 %collective-permute-start.5 = (bf16[2,8,32,256]{3,2,1,0:T(8,128)(2,1)S(1)}, bf16[2,8,32,256]{3,2,1,0:T(8,128)(2,1)S(1)}, u32[]{:S(2)}, u32[]{:S(2)}) collective-permute-start(bf16[2,8,32,256]{3,2,1,0:T(8,128)(2,1)S(1)} %get-tuple-element.49), channel_id=1, source_target_pairs={{0,2},{2,4},{4,6},{6,8},{8,10},{10,12},{12,14},{14,0},{1,3},{3,5},... | collective-permute-start | bytes 786440 | tf_op jit(solution)/shard_map/ppermute | solution.py:17
  40.6 6.4 %collective-permute-start.6 = (bf16[2,8,32,256]{3,2,1,0:T(8,128)(2,1)S(1)}, bf16[2,8,32,256]{3,2,1,0:T(8,128)(2,1)}, u32[]{:S(2)}, u32[]{:S(2)}) collective-permute-start(bf16[2,8,32,256]{3,2,1,0:T(8,128)(2,1)S(1)} %get-tuple-element.52), channel_id=1, source_target_pairs={{0,14},{2,0},{4,2},{6,4},{8,6},{10,8},{12,10},{14,12},{1,15},{3,1}... | collective-permute-start | bytes 786440 | tf_op jit(solution)/shard_map/ppermute | solution.py:17
  41.0 6.8 %collective-permute-start.7 = (bf16[2,8,32,256]{3,2,1,0:T(8,128)(2,1)S(1)}, bf16[2,8,32,256]{3,2,1,0:T(8,128)(2,1)}, u32[]{:S(2)}, u32[]{:S(2)}) collective-permute-start(bf16[2,8,32,256]{3,2,1,0:T(8,128)(2,1)S(1)} %get-tuple-element.53), channel_id=1, source_target_pairs={{0,2},{2,4},{4,6},{6,8},{8,10},{10,12},{12,14},{14,0},{1,3},{3,5},... | collective-permute-start | bytes 786440 | tf_op jit(solution)/shard_map/ppermute | solution.py:17
  43.3 5.7 %collective-permute-start.8 = (bf16[2,256,256]{2,1,0:T(8,128)(2,1)S(1)}, bf16[2,256,256]{2,1,0:T(8,128)(2,1)S(1)}, u32[]{:S(2)}, u32[]{:S(2)}) collective-permute-start(bf16[2,256,256]{2,1,0:T(8,128)(2,1)S(1)} %get-tuple-element.85), channel_id=1, source_target_pairs={{0,1},{1,0},{2,3},{3,2},{4,5},{5,4},{6,7},{7,6},{8,9},{9,8},{10,11... | collective-permute-start | bytes 786440 | tf_op jit(solution)/shard_map/ppermute | solution.py:17
  49.0 11.8 %copy-start.5 = (bf16[8,2,256,256]{3,2,1,0:T(8,128)(2,1)S(1)}, bf16[8,2,256,256]{3,2,1,0:T(8,128)(2,1)}, u32[]{:S(2)}) copy-start(bf16[8,2,256,256]{3,2,1,0:T(8,128)(2,1)} %refs_0_.2) | copy-start | bytes 6291460
  49.0 12.0 %copy-start.13 = (bf16[2,256,256]{2,1,0:T(8,128)(2,1)}, bf16[2,256,256]{2,1,0:T(8,128)(2,1)S(1)}, u32[]{:S(2)}) copy-start(bf16[2,256,256]{2,1,0:T(8,128)(2,1)S(1)} %collective-permute-done.8) | copy-start | bytes 786436
  51.4 36.7 %collective-permute-start.11 = (bf16[16,256,256]{2,1,0:T(8,128)(2,1)}, bf16[16,256,256]{2,1,0:T(8,128)(2,1)}, u32[]{:S(2)}, u32[]{:S(2)}) collective-permute-start(bf16[16,256,256]{2,1,0:T(8,128)(2,1)} %all-to-all-done.e_ref), channel_id=1, source_target_pairs={{0,1},{1,0},{2,3},{3,2},{4,5},{5,4},{6,7},{7,6},{8,9},{9,8},{10,11... | collective-permute-start | bytes 6291464 | tf_op jit(solution)/shard_map/ppermute | solution.py:17
  55.6 15.2 %all-to-all-start.2 = ((bf16[16,64,256]{2,1,0:T(8,128)(2,1)}), bf16[16,64,256]{2,1,0:T(8,128)(2,1)S(1)}, u32[]{:S(2)}, u32[]{:S(2)}) async-start(bf16[16,64,256]{2,1,0:T(8,128)(2,1)} %bitcast.8), calls=%async_computation.2 | async-start | bytes 1048576 | tf_op jit(solution)/shard_map/all_to_all | solution.py:187
  70.9 36.4 %all-to-all-start.1 = ((bf16[16,256,256]{2,1,0:T(8,128)(2,1)}), bf16[16,256,256]{2,1,0:T(8,128)(2,1)}, u32[]{:S(2)}, u32[]{:S(2)}) async-start(bf16[16,256,256]{2,1,0:T(8,128)(2,1)} %bitcast.56), calls=%async_computation.1 | async-start | bytes 4194304 | tf_op jit(solution)/shard_map/all_to_all | solution.py:186
  75.6 12.5 %collective-permute-start.9 = (bf16[32,32,256]{2,1,0:T(8,128)(2,1)S(1)}, bf16[32,32,256]{2,1,0:T(8,128)(2,1)S(1)}, u32[]{:S(2)}, u32[]{:S(2)}) collective-permute-start(bf16[32,32,256]{2,1,0:T(8,128)(2,1)S(1)} %bitcast.52), channel_id=1, source_target_pairs={{0,2},{2,4},{4,6},{6,8},{8,10},{10,12},{12,14},{14,0},{1,3},{3,5},... | collective-permute-start | bytes 1572872 | tf_op jit(solution)/shard_map/ppermute | solution.py:17
  75.9 12.2 %collective-permute-start.10 = (bf16[32,32,256]{2,1,0:T(8,128)(2,1)S(1)}, bf16[32,32,256]{2,1,0:T(8,128)(2,1)S(1)}, u32[]{:S(2)}, u32[]{:S(2)}) collective-permute-start(bf16[32,32,256]{2,1,0:T(8,128)(2,1)S(1)} %bitcast.53), channel_id=1, source_target_pairs={{0,14},{2,0},{4,2},{6,4},{8,6},{10,8},{12,10},{14,12},{1,15},{3,1}... | collective-permute-start | bytes 1572872 | tf_op jit(solution)/shard_map/ppermute | solution.py:17
  78.4 12.5 %copy-start.14 = (bf16[2,256,256]{2,1,0:T(8,128)(2,1)S(1)}, bf16[2,256,256]{2,1,0:T(8,128)(2,1)}, u32[]{:S(2)}) copy-start(bf16[2,256,256]{2,1,0:T(8,128)(2,1)} %copy-done.13) | copy-start | bytes 786436
  88.1 7.2 %copy-start.9 = (bf16[32,32,256]{2,1,0:T(8,128)(2,1)}, bf16[32,32,256]{2,1,0:T(8,128)(2,1)S(1)}, u32[]{:S(2)}) copy-start(bf16[32,32,256]{2,1,0:T(8,128)(2,1)S(1)} %collective-permute-done.10.refs_5_.refs_7_) | copy-start | bytes 1572868
  88.1 11.7 %collective-permute-start.12 = (bf16[32,32,256]{2,1,0:T(8,128)(2,1)S(1)}, bf16[32,32,256]{2,1,0:T(8,128)(2,1)}, u32[]{:S(2)}, u32[]{:S(2)}) collective-permute-start(bf16[32,32,256]{2,1,0:T(8,128)(2,1)S(1)} %collective-permute-done.9.refs_4_.refs_6_), channel_id=1, source_target_pairs={{0,2},{2,4},{4,6},{6,8},{8,10},{10,12},{12,14},{14,0},{1,3},{3,5},... | collective-permute-start | bytes 1572872 | tf_op jit(solution)/shard_map/ppermute | solution.py:17
  88.2 11.6 %collective-permute-start.13 = (bf16[32,32,256]{2,1,0:T(8,128)(2,1)S(1)}, bf16[32,32,256]{2,1,0:T(8,128)(2,1)}, u32[]{:S(2)}, u32[]{:S(2)}) collective-permute-start(bf16[32,32,256]{2,1,0:T(8,128)(2,1)S(1)} %collective-permute-done.10.refs_5_.refs_7_), channel_id=1, source_target_pairs={{0,14},{2,0},{4,2},{6,4},{8,6},{10,8},{12,10},{14,12},{1,15},{3,1}... | collective-permute-start | bytes 1572872 | tf_op jit(solution)/shard_map/ppermute | solution.py:17
  99.8 10.9 %collective-permute-start.14 = (bf16[32,32,256]{2,1,0:T(8,128)(2,1)}, bf16[32,32,256]{2,1,0:T(8,128)(2,1)}, u32[]{:S(2)}, u32[]{:S(2)}) collective-permute-start(bf16[32,32,256]{2,1,0:T(8,128)(2,1)} %collective-permute-done.12.refs_6_.refs_8_), channel_id=1, source_target_pairs={{0,2},{2,4},{4,6},{6,8},{8,10},{10,12},{12,14},{14,0},{1,3},{3,5},... | collective-permute-start | bytes 1572872 | tf_op jit(solution)/shard_map/ppermute | solution.py:17
  99.8 10.9 %collective-permute-start.15 = (bf16[32,32,256]{2,1,0:T(8,128)(2,1)}, bf16[32,32,256]{2,1,0:T(8,128)(2,1)}, u32[]{:S(2)}, u32[]{:S(2)}) collective-permute-start(bf16[32,32,256]{2,1,0:T(8,128)(2,1)} %collective-permute-done.13.refs_7_.refs_9_), channel_id=1, source_target_pairs={{0,14},{2,0},{4,2},{6,4},{8,6},{10,8},{12,10},{14,12},{1,15},{3,1}... | collective-permute-start | bytes 1572872 | tf_op jit(solution)/shard_map/ppermute | solution.py:17
  102.6 1.6 %copy-start.2 = (bf16[256,16,256]{2,1,0:T(8,128)(2,1)S(1)}, bf16[256,16,256]{2,1,0:T(8,128)(2,1)}, u32[]{:S(2)}) copy-start(bf16[256,16,256]{2,1,0:T(8,128)(2,1)} %copy-done.1) | copy-start | bytes 6291460
  110.7 9.5 %collective-permute-start.17 = (bf16[16,256,256]{2,1,0:T(8,128)(2,1)}, bf16[16,256,256]{2,1,0:T(8,128)(2,1)}, u32[]{:S(2)}, u32[]{:S(2)}) collective-permute-start(bf16[16,256,256]{2,1,0:T(8,128)(2,1)} %all-to-all-done.1.e_ref), channel_id=1, source_target_pairs={{0,1},{1,0},{2,3},{3,2},{4,5},{5,4},{6,7},{7,6},{8,9},{9,8},{10,11... | collective-permute-start | bytes 6291464 | tf_op jit(solution)/shard_map/ppermute | solution.py:17
  115.7 14.7 %collective-permute-start.16 = (bf16[32,32,256]{2,1,0:T(8,128)(2,1)}, bf16[32,32,256]{2,1,0:T(8,128)(2,1)}, u32[]{:S(2)}, u32[]{:S(2)}) collective-permute-start(bf16[32,32,256]{2,1,0:T(8,128)(2,1)} %collective-permute-done.14.refs_10_), channel_id=1, source_target_pairs={{0,2},{2,4},{4,6},{6,8},{8,10},{10,12},{12,14},{14,0},{1,3},{3,5},... | collective-permute-start | bytes 1572872 | tf_op jit(solution)/shard_map/ppermute | solution.py:17
  120.2 4.6 %copy-start.3 = (bf16[256,16,256]{2,1,0:T(8,128)(2,1)S(1)}, bf16[256,16,256]{2,1,0:T(8,128)(2,1)}, u32[]{:S(2)}) copy-start(bf16[256,16,256]{2,1,0:T(8,128)(2,1)} %copy-done.1) | copy-start | bytes 6291460
  120.3 4.6 %copy-start.11 = (bf16[32,32,256]{2,1,0:T(8,128)(2,1)S(1)}, bf16[32,32,256]{2,1,0:T(8,128)(2,1)}, u32[]{:S(2)}) copy-start(bf16[32,32,256]{2,1,0:T(8,128)(2,1)} %copy-done.9) | copy-start | bytes 1572868
  132.8 15.2 %all-to-all-start.3 = ((f32[32,8,128]{2,1,0:T(8,128)}), f32[32,8,128]{2,1,0:T(8,128)S(1)}, u32[]{:S(2)}, u32[]{:S(2)}) async-start(f32[32,8,128]{2,1,0:T(8,128)} %bitcast.24), calls=%async_computation.3 | async-start | bytes 262144 | tf_op jit(solution)/shard_map/all_to_all | solution.py:217
  (5 other events, 6.7 us)

commit v3 on v2

--- a/solution.py
+++ b/solution.py
@@ -30,7 +30,7 @@
         w_ref[:, :, part * LANES : (part + 1) * LANES] = wide[part].reshape(modes, ops, LANES).astype(BF16)
 
 
-def sandwiches(elements, prop):
+def sandwiches(elements, prop, flops=None):
     ops, modes, _ = elements.shape
     return pl.pallas_call(
         sandwich_kernel,
@@ -38,44 +38,38 @@
         scratch_shapes=[pltpu.VMEM((modes // LANES, modes * ops, LANES), F32)],
         compiler_params=pltpu.CompilerParams(vmem_limit_bytes=16 * 2**20),
         cost_estimate=pl.CostEstimate(
-            flops=4 * ops * modes**3, bytes_accessed=4 * ops * modes**2, transcendentals=0
+            flops=4 * ops * modes**3 if flops is None else flops,
+            bytes_accessed=4 * ops * modes**2 if flops is None else flops,
+            transcendentals=0,
         ),
     )(elements, prop)
 
 
-def double_kernel(time, e_ref, o_ref, held, get_sem, put_sem):
-    get = pltpu.make_async_copy(e_ref.at[:, time], held, get_sem)
-    puts = [pltpu.make_async_copy(held, o_ref.at[:, twin], put_sem.at[twin]) for twin in range(2)]
-    get.start()
-    get.wait()
+def double_kernel(time, e_ref, o_ref, sem):
+    puts = [pltpu.make_async_copy(e_ref.at[:, time], o_ref.at[:, twin], sem.at[twin]) for twin in range(2)]
     for put in puts:
         put.start()
     for put in puts:
         put.wait()
 
 
-def doubled(elements, time, limit):
+def doubled(elements, time):
     ops, _, modes, _ = elements.shape
     out = pl.pallas_call(
         lambda *refs: double_kernel(time, *refs),
-        in_specs=[pl.BlockSpec(memory_space=pl.ANY)],
+        in_specs=[pl.BlockSpec(memory_space=pltpu.VMEM)],
         out_specs=pl.BlockSpec(memory_space=pl.ANY),
         out_shape=jax.ShapeDtypeStruct((ops, 2, modes, modes), BF16),
-        scratch_shapes=[
-            pltpu.VMEM((ops, modes, modes), BF16),
-            pltpu.SemaphoreType.DMA(()),
-            pltpu.SemaphoreType.DMA((2,)),
-        ],
-        compiler_params=pltpu.CompilerParams(vmem_limit_bytes=limit * 2**20),
+        scratch_shapes=[pltpu.SemaphoreType.DMA((2,))],
+        compiler_params=pltpu.CompilerParams(vmem_limit_bytes=8 * 2**20),
         cost_estimate=pl.CostEstimate(flops=2**32, bytes_accessed=6 * ops * modes**2, transcendentals=0),
     )(elements)
     return out.reshape(2 * ops, modes, modes)
 
 
-def slot_kernel(when_ref, own_ref, other_ref, o_ref, zeros, sem):
+def slot_kernel(when_ref, own_ref, other_ref, o_ref, sem):
     z, core = lax.axis_index("z"), lax.axis_index("c")
     times, count = own_ref.shape[1], o_ref.shape[0]
-    zeros[...] = jnp.zeros_like(zeros)
     for slot in range(count):
         when = when_ref[2 * slot + core]
         holder, inside = when // times, when % times
@@ -83,13 +77,16 @@
         mine = here & (holder % 2 == core)
 
         def fetch(source, slot=slot):
-            pltpu.make_async_copy(source, o_ref.at[slot], sem.at[slot]).start()
+            copy = pltpu.make_async_copy(source, o_ref.at[slot], sem.at[slot])
+            copy.start()
+            copy.wait()
+
+        def clear(slot=slot):
+            o_ref[slot] = jnp.zeros_like(o_ref[slot])
 
         pl.when(mine)(lambda inside=inside, fetch=fetch: fetch(own_ref.at[:, inside]))
         pl.when(here & ~mine)(lambda inside=inside, fetch=fetch: fetch(other_ref.at[:, inside]))
-        pl.when(~here)(lambda fetch=fetch: fetch(zeros))
-    for slot in range(count):
-        pltpu.make_async_copy(zeros, o_ref.at[slot], sem.at[slot]).wait()
+        pl.when(~here)(clear)
 
 
 def slots_of(src_times, own, other):
@@ -97,10 +94,10 @@
     count = src_times.shape[0] // 2
     return pl.pallas_call(
         slot_kernel,
-        in_specs=[pl.BlockSpec(memory_space=pltpu.SMEM)] + [pl.BlockSpec(memory_space=pl.ANY)] * 2,
+        in_specs=[pl.BlockSpec(memory_space=pltpu.SMEM)] + [pl.BlockSpec(memory_space=pltpu.VMEM)] * 2,
         out_specs=pl.BlockSpec(memory_space=pltpu.VMEM),
         out_shape=jax.ShapeDtypeStruct((count, ops, modes, modes), BF16),
-        scratch_shapes=[pltpu.VMEM((ops, modes, modes), BF16), pltpu.SemaphoreType.DMA((count,))],
+        scratch_shapes=[pltpu.SemaphoreType.DMA((count,))],
         compiler_params=pltpu.CompilerParams(vmem_limit_bytes=8 * 2**20),
     )(src_times, own, other)
 
@@ -157,7 +154,7 @@
     props_near = lax.dynamic_index_in_dim(perambulators, my_k, 1, keepdims=False)
     props_far = lax.dynamic_index_in_dim(perambulators, 2 * k_half + 1 - core, 1, keepdims=False)
 
-    double = doubled(elementals, 0, 60)
+    double = doubled(elementals, 0)
 
     beside = shift(elementals, "c", 1)
     beside, double = tie(beside, double)
@@ -175,17 +172,21 @@
             send_up = send_up + up
         send_down, send_up = tie(send_down, send_up)
         down, up = shift(send_down, "z", -1), shift(send_up, "z", 1)
-        down, up = tie(down, up)
+        if step == 2:
+            double = doubled(elementals, 1)
+            down, up, double = tie(down, up, double)
+        else:
+            down, up = tie(down, up)
     mine = chunk(z) + up + down
     props_far = shift(props_far, "c", 1)
     first, mine, props_near, props_far = tie(first, mine, props_near, props_far)
 
     mine = mine.reshape(2, 2, CLASSES, rows, modes).transpose(2, 0, 1, 3, 4)
     mine = jnp.broadcast_to(mine[None], (2,) + mine.shape).reshape(chips, 2 * rows, modes)
-    elements, mine = tie(elementals, mine)
-    second = lax.all_to_all(doubled(elements, 1, 8), xy, 0, 0, tiled=True)
     mine = lax.all_to_all(mine, xy, 0, 0, tiled=True)
     mine = mine.reshape(2 * chips, rows, modes).transpose(1, 0, 2)
+    double, mine = tie(double, mine)
+    second = lax.all_to_all(double, xy, 0, 0, tiled=True)
 
     first_far = shift(first, "c", 1)
     number = lambda offset: (z + planes + offset) % planes
@@ -201,11 +202,13 @@
     w_first = w_near, w_far
     up, down = shift(up, "z", 1), shift(down, "z", -1)
     (early,) = block_products([(w_first, range(5))], found)
-    second, up, down, early = tie(second, up, down, early)
+    up, down, early = tie(up, down, early)
+    ring = [(2 * i + c, 2 * ((i + (-1) ** c) % planes) + c) for i in range(planes) for c in range(2)]
+    last = lax.ppermute(jnp.where(core == 0, up, down), ("z", "c"), ring)
+    second, up, down = tie(second, up, down)
     found += [(number(-3), up), (number(3), down)]
-    last = shift(up, "z", 1)
     second_far = shift(second, "c", 1)
-    w_second = sandwiches(second, props_near[1]), sandwiches(second_far, props_far[1])
+    w_second = sandwiches(second, props_near[1], 1), sandwiches(second_far, props_far[1], 1)
     middle, total = block_products([(w_first, range(5, 7)), (w_second, range(7))], found)
     last, middle = tie(last, middle)
     late = block_products([(w_first, [0]), (w_second, [0])], [(number(reach), last)])

time: 151 us -> 148 us (0.980)
  waiting for transfers between devices: 47.9 us -> 32.2 us
  blocking collectives: 0 us -> 15 us
  starting transfers between devices: 56.3 us -> 53.3 us
  Pallas kernels: 27.9 us -> 25.2 us
  local copies, waits for them, and re-layouts: 14.4 us -> 16.3 us
    all_to_all x0 -> x1, blocking collectives: none -> 15 us  [per_device(): mine = lax.all_to_all(mine, xy, 0, 0, tiled=True)]
    all_to_all x2 -> x1, waiting for transfers between devices: 8.5 us -> 0.01 us  [per_device(): second = lax.all_to_all(double, xy, 0, 0, tiled=True)]
    ppermute x18 -> x17, waiting for transfers between devices: 30 us -> 22.8 us  [shift(): lax.ppermute(block, axis, [(i, (i + step) % size) for i in range(size)])]
    all_to_all x2 -> x1, starting transfers between devices: 9.5 us -> 4.45 us  [per_device(): second = lax.all_to_all(double, xy, 0, 0, tiled=True)]
    ppermute x0 -> x1, starting transfers between devices: none -> 3.07 us  [per_device(): last = lax.ppermute(jnp.where(core == 0, up, down), ('z', 'c'), ring)]
    unnamed x30 -> x32, local copies, waits for them, and re-layouts: 9.86 us -> 12.5 us
    ppermute x18 -> x17, starting transfers between devices: 32.4 us -> 32.4 us  [shift(): lax.ppermute(block, axis, [(i, (i + step) % size) for i in range(size)])]
  transfers between devices with their start and end apart: 22 -> 21, of which waited for: 13 -> 11; matrix products, arithmetic and copies ran while one was open for 3% -> 3% of each run, Pallas kernels for 17% -> 16%
where the time goes in v3:
time: 148 us; the launch traced here: 147 us
  starting transfers between devices  53.3 us (36%)
  waiting for transfers between devices  32.2 us (22%)
  Pallas kernels  25.2 us (17%)
  local copies, waits for them, and re-layouts  16.3 us (11%)
  blocking collectives  15 us (10%)
  other arithmetic  4.12 us (3%)
    ppermute x17, starting transfers between devices, shift(): lax.ppermute(block, axis, [(i, (i + step) % size) for i in range(size)])  32.4 us
    ppermute x17, waiting for transfers between devices, shift(): lax.ppermute(block, axis, [(i, (i + step) % size) for i in range(size)])  22.8 us
    pallas_call x4, Pallas kernels, sandwiches(): pl.pallas_call(sandwich_kernel, out_shape=jax.ShapeDtypeStruct((modes, op...  17.7 us
    all_to_all x1, blocking collectives, per_device(): mine = lax.all_to_all(mine, xy, 0, 0, tiled=True)  15 us
    unnamed x32, local copies, waits for them, and re-layouts  12.5 us
    all_to_all x1, waiting for transfers between devices, per_device(): out = lax.all_to_all(out, ('x', 'y', 'c'), 0, 0, tiled=True)  6.92 us
    all_to_all x1, starting transfers between devices, per_device(): first = lax.all_to_all(double, xy, 0, 0, tiled=True)  6.81 us
    all_to_all x1, starting transfers between devices, per_device(): out = lax.all_to_all(out, ('x', 'y', 'c'), 0, 0, tiled=True)  6.5 us
  transfers between devices with their start and end apart: 21, of which 11 were waited for; matrix products, arithmetic and copies ran while one was open for 3% of the time, Pallas kernels for 16%

profile of v3, /device:TPU:1, one launch (start us, length us, event | category | flops | bytes accessed | tf_op | source)
XLA Modules:
  0.0 147.0 jit_solution(14543740839234905766)
XLA Ops:
  0.0 3.2 %collective-permute-start = (bf16[8,2,256,256]{3,2,1,0:T(8,128)(2,1)}, bf16[8,2,256,256]{3,2,1,0:T(8,128)(2,1)S(1)}, u32[]{:S(2)}, u32[]{:S(2)}) collective-permute-start(bf16[8,2,256,256]{3,2,1,0:T(8,128)(2,1)} %refs_0_.3), channel_id=1, source_target_pairs={{0,1},{1,0},{2,3},{3,2},{4,5},{5,4},{6,7},{7,6},{8,9},{9,8},{10,11... | collective-permute-start | bytes 6291464 | tf_op jit(solution)/shard_map/ppermute | solution.py:17
  3.2 1.6 %copy-done.4 = bf16[8,2,256,256]{3,2,1,0:T(8,128)(2,1)S(1)} copy-done((bf16[8,2,256,256]{3,2,1,0:T(8,128)(2,1)S(1)}, bf16[8,2,256,256]{3,2,1,0:T(8,128)(2,1)}, u32[]{:S(2)}) %copy-start.4) | copy-done | bytes 2097176
  8.6 1.6 %copy-done.7 = bf16[8,2,256,256]{3,2,1,0:T(8,128)(2,1)S(1)} copy-done((bf16[8,2,256,256]{3,2,1,0:T(8,128)(2,1)S(1)}, bf16[8,2,256,256]{3,2,1,0:T(8,128)(2,1)}, u32[]{:S(2)}) %copy-start.7) | copy-done | bytes 2097176
  11.0 3.9 %collective-permute-start.1 = (bf16[2,8,32,256]{3,2,1,0:T(8,128)(2,1)S(1)}, bf16[2,8,32,256]{3,2,1,0:T(8,128)(2,1)S(1)}, u32[]{:S(2)}, u32[]{:S(2)}) collective-permute-start(bf16[2,8,32,256]{3,2,1,0:T(8,128)(2,1)S(1)} %get-tuple-element.90), channel_id=1, source_target_pairs={{0,14},{2,0},{4,2},{6,4},{8,6},{10,8},{12,10},{14,12},{1,15},{3,1}... | collective-permute-start | bytes 786440 | tf_op jit(solution)/shard_map/ppermute | solution.py:17
  14.9 6.8 %all-to-all-start = ((bf16[16,256,256]{2,1,0:T(8,128)(2,1)}), bf16[16,256,256]{2,1,0:T(8,128)(2,1)}, u32[]{:S(2)}, u32[]{:S(2)}) async-start(bf16[16,256,256]{2,1,0:T(8,128)(2,1)} %bitcast.56), calls=%async_computation | async-start | bytes 4194304 | tf_op jit(solution)/shard_map/all_to_all | solution.py:166
  21.8 2.0 %collective-permute-start.2 = (bf16[2,8,32,256]{3,2,1,0:T(8,128)(2,1)S(1)}, bf16[2,8,32,256]{3,2,1,0:T(8,128)(2,1)S(1)}, u32[]{:S(2)}, u32[]{:S(2)}) collective-permute-start(bf16[2,8,32,256]{3,2,1,0:T(8,128)(2,1)S(1)} %dynamic-slice_add_fusion.3), channel_id=1, source_target_pairs={{0,14},{2,0},{4,2},{6,4},{8,6},{10,8},{12,10},{14,12},{1,15},{3,1}... | collective-permute-start | bytes 786440 | tf_op jit(solution)/shard_map/ppermute | solution.py:17
  23.8 5.1 %collective-permute-done.2 = bf16[2,8,32,256]{3,2,1,0:T(8,128)(2,1)S(1)} collective-permute-done((bf16[2,8,32,256]{3,2,1,0:T(8,128)(2,1)S(1)}, bf16[2,8,32,256]{3,2,1,0:T(8,128)(2,1)S(1)}, u32[]{:S(2)}, u32[]{:S(2)}) %collective-permute-start.2) | collective-permute-done | bytes 262176 | tf_op jit(solution)/shard_map/ppermute | solution.py:17
  28.9 2.5 %collective-permute-done.3 = bf16[2,8,32,256]{3,2,1,0:T(8,128)(2,1)S(1)} collective-permute-done((bf16[2,8,32,256]{3,2,1,0:T(8,128)(2,1)S(1)}, bf16[2,8,32,256]{3,2,1,0:T(8,128)(2,1)S(1)}, u32[]{:S(2)}, u32[]{:S(2)}) %collective-permute-start.3) | collective-permute-done | bytes 262176 | tf_op jit(solution)/shard_map/ppermute | solution.py:17
  33.2 1.6 %copy-done.5 = bf16[8,2,256,256]{3,2,1,0:T(8,128)(2,1)S(1)} copy-done((bf16[8,2,256,256]{3,2,1,0:T(8,128)(2,1)S(1)}, bf16[8,2,256,256]{3,2,1,0:T(8,128)(2,1)}, u32[]{:S(2)}) %copy-start.5) | copy-done | bytes 2097176
  37.3 1.5 %collective-permute-done.5 = bf16[2,8,32,256]{3,2,1,0:T(8,128)(2,1)S(1)} collective-permute-done((bf16[2,8,32,256]{3,2,1,0:T(8,128)(2,1)S(1)}, bf16[2,8,32,256]{3,2,1,0:T(8,128)(2,1)S(1)}, u32[]{:S(2)}, u32[]{:S(2)}) %collective-permute-start.5) | collective-permute-done | bytes 262176 | tf_op jit(solution)/shard_map/ppermute | solution.py:17
  41.6 3.7 %collective-permute-start.8 = (bf16[2,256,256]{2,1,0:T(8,128)(2,1)S(1)}, bf16[2,256,256]{2,1,0:T(8,128)(2,1)S(1)}, u32[]{:S(2)}, u32[]{:S(2)}) collective-permute-start(bf16[2,256,256]{2,1,0:T(8,128)(2,1)S(1)} %get-tuple-element.91), channel_id=1, source_target_pairs={{0,1},{1,0},{2,3},{3,2},{4,5},{5,4},{6,7},{7,6},{8,9},{9,8},{10,11... | collective-permute-start | bytes 786440 | tf_op jit(solution)/shard_map/ppermute | solution.py:17
  47.3 2.5 %all-to-all-done.e_ref = bf16[16,256,256]{2,1,0:T(8,128)(2,1)} async-done(((bf16[16,256,256]{2,1,0:T(8,128)(2,1)}), bf16[16,256,256]{2,1,0:T(8,128)(2,1)}, u32[]{:S(2)}, u32[]{:S(2)}) %all-to-all-start) | async-done | bytes 2097184 | tf_op jit(solution)/shard_map/all_to_all | solution.py:166
  49.8 3.3 %collective-permute-start.11 = (bf16[16,256,256]{2,1,0:T(8,128)(2,1)}, bf16[16,256,256]{2,1,0:T(8,128)(2,1)}, u32[]{:S(2)}, u32[]{:S(2)}) collective-permute-start(bf16[16,256,256]{2,1,0:T(8,128)(2,1)} %all-to-all-done.e_ref), channel_id=1, source_target_pairs={{0,1},{1,0},{2,3},{3,2},{4,5},{5,4},{6,7},{7,6},{8,9},{9,8},{10,11... | collective-permute-start | bytes 6291464 | tf_op jit(solution)/shard_map/ppermute | solution.py:17
  53.2 15.0 %all_to_all.20 = bf16[16,64,256]{2,1,0:T(8,128)(2,1)S(1)} all-to-all(bf16[16,64,256]{2,1,0:T(8,128)(2,1)S(1)} %bitcast.58), channel_id=1, replica_groups=mesh['x'=4,'y'=4,'z'=8,'c'=2] {'x','y'}, dimensions={0} | all-to-all | bytes 1048576 | tf_op jit(solution)/shard_map/all_to_all | solution.py:186
  68.5 4.4 %all-to-all-start.2 = ((bf16[16,256,256]{2,1,0:T(8,128)(2,1)}), bf16[16,256,256]{2,1,0:T(8,128)(2,1)}, u32[]{:S(2)}, u32[]{:S(2)}) async-start(bf16[16,256,256]{2,1,0:T(8,128)(2,1)} %bitcast.4), calls=%async_computation.2 | async-start | bytes 4194304 | tf_op jit(solution)/shard_map/all_to_all | solution.py:189
  73.3 2.4 %collective-permute-start.10 = (bf16[32,32,256]{2,1,0:T(8,128)(2,1)S(1)}, bf16[32,32,256]{2,1,0:T(8,128)(2,1)S(1)}, u32[]{:S(2)}, u32[]{:S(2)}) collective-permute-start(bf16[32,32,256]{2,1,0:T(8,128)(2,1)S(1)} %bitcast.53), channel_id=1, source_target_pairs={{0,14},{2,0},{4,2},{6,4},{8,6},{10,8},{12,10},{14,12},{1,15},{3,1}... | collective-permute-start | bytes 1572872 | tf_op jit(solution)/shard_map/ppermute | solution.py:17
  75.7 4.4 %shard_map.58.refs_1_ = bf16[256,16,256]{2,1,0:T(8,128)(2,1)S(1)} custom-call(bf16[16,256,256]{2,1,0:T(8,128)(2,1)} %all-to-all-done.e_ref, bf16[256,256]{1,0:T(8,128)(2,1)S(1)} %get-tuple-element.96.p_ref), custom_call_target="tpu_custom_call" | custom-call | flops 1073741824 | bytes 4194304 | tf_op jit(solution)/shard_map/pallas_call | solution.py:35
  80.1 5.3 %collective-permute-done.9.refs_4_.refs_6_ = bf16[32,32,256]{2,1,0:T(8,128)(2,1)S(1)} collective-permute-done((bf16[32,32,256]{2,1,0:T(8,128)(2,1)S(1)}, bf16[32,32,256]{2,1,0:T(8,128)(2,1)S(1)}, u32[]{:S(2)}, u32[]{:S(2)}) %collective-permute-start.9) | collective-permute-done | bytes 524320 | tf_op jit(solution)/shard_map/ppermute | solution.py:17
  85.5 2.7 %collective-permute-start.13 = (bf16[32,32,256]{2,1,0:T(8,128)(2,1)S(1)}, bf16[32,32,256]{2,1,0:T(8,128)(2,1)}, u32[]{:S(2)}, u32[]{:S(2)}) collective-permute-start(bf16[32,32,256]{2,1,0:T(8,128)(2,1)S(1)} %collective-permute-done.10.refs_5_.refs_7_), channel_id=1, source_target_pairs={{0,14},{2,0},{4,2},{6,4},{8,6},{10,8},{12,10},{14,12},{1,15},{3,1}... | collective-permute-start | bytes 1572872 | tf_op jit(solution)/shard_map/ppermute | solution.py:17
  88.2 4.4 %shard_map.59.refs_2_ = bf16[256,16,256]{2,1,0:T(8,128)(2,1)S(1)} custom-call(bf16[16,256,256]{2,1,0:T(8,128)(2,1)} %collective-permute-done.11.e_ref, bf16[256,256]{1,0:T(8,128)(2,1)S(1)} %get-tuple-element.94.p_ref), custom_call_target="tpu_custom_call" | custom-call | flops 1073741824 | bytes 4194304 | tf_op jit(solution)/shard_map/pallas_call | solution.py:35
  94.0 3.1 %collective-permute-done.12.refs_6_.refs_8_ = bf16[32,32,256]{2,1,0:T(8,128)(2,1)} collective-permute-done((bf16[32,32,256]{2,1,0:T(8,128)(2,1)S(1)}, bf16[32,32,256]{2,1,0:T(8,128)(2,1)}, u32[]{:S(2)}, u32[]{:S(2)}) %collective-permute-start.12) | collective-permute-done | bytes 524320 | tf_op jit(solution)/shard_map/ppermute | solution.py:17
  97.1 2.7 %collective-permute-start.15 = (bf16[32,32,256]{2,1,0:T(8,128)(2,1)}, bf16[32,32,256]{2,1,0:T(8,128)(2,1)}, u32[]{:S(2)}, u32[]{:S(2)}) collective-permute-start(bf16[32,32,256]{2,1,0:T(8,128)(2,1)} %collective-permute-done.13.refs_7_.refs_9_), channel_id=1, source_target_pairs={{0,14},{2,0},{4,2},{6,4},{8,6},{10,8},{12,10},{14,12},{1,15},{3,1}... | collective-permute-start | bytes 1572872 | tf_op jit(solution)/shard_map/ppermute | solution.py:17
  99.9 1.6 %copy-done.2 = bf16[256,16,256]{2,1,0:T(8,128)(2,1)S(1)} copy-done((bf16[256,16,256]{2,1,0:T(8,128)(2,1)S(1)}, bf16[256,16,256]{2,1,0:T(8,128)(2,1)}, u32[]{:S(2)}) %copy-start.2) | copy-done | bytes 2097176
  103.6 2.0 %shard_map.60 = f32[32,32]{1,0:T(8,128)S(1)} custom-call(s32[5]{0:T(128)S(1)} %stack.43.refs_0_, bf16[256,16,256]{2,1,0:T(8,128)(2,1)S(1)} %shard_map.58.refs_1_, bf16[256,16,256]{2,1,0:T(8,128)(2,1)S(1)} %copy-done.2, bf16[32,32,256]{2,1,0:T(8,128)(2,1)S(1)} %bitcast.54, bf16[32,32,256]{2,1,0:T(8,128)(2,1)S(1)} %copy-done.10, ...), custom_call_target="tpu_custom_call" | custom-call | flops 83886080 | bytes 5242880 | tf_op jit(solution)/shard_map/pallas_call | solution.py:124
  105.6 2.3 %collective-permute-done.14.refs_10_ = bf16[32,32,256]{2,1,0:T(8,128)(2,1)S(1)} collective-permute-done((bf16[32,32,256]{2,1,0:T(8,128)(2,1)}, bf16[32,32,256]{2,1,0:T(8,128)(2,1)S(1)}, u32[]{:S(2)}, u32[]{:S(2)}) %collective-permute-start.14) | collective-permute-done | bytes 524320 | tf_op jit(solution)/shard_map/ppermute | solution.py:17
  107.9 5.0 %collective-permute-start.17 = (bf16[16,256,256]{2,1,0:T(8,128)(2,1)}, bf16[16,256,256]{2,1,0:T(8,128)(2,1)}, u32[]{:S(2)}, u32[]{:S(2)}) collective-permute-start(bf16[16,256,256]{2,1,0:T(8,128)(2,1)} %all-to-all-done.2.e_ref), channel_id=1, source_target_pairs={{0,1},{1,0},{2,3},{3,2},{4,5},{5,4},{6,7},{7,6},{8,9},{9,8},{10,11... | collective-permute-start | bytes 6291464 | tf_op jit(solution)/shard_map/ppermute | solution.py:17
  114.1 3.1 %collective-permute-start.16 = (bf16[32,32,256]{2,1,0:T(8,128)(2,1)S(1)}, bf16[32,32,256]{2,1,0:T(8,128)(2,1)S(1)}, u32[]{:S(2)}, u32[]{:S(2)}) collective-permute-start(bf16[32,32,256]{2,1,0:T(8,128)(2,1)S(1)} %broadcast_select_fusion), channel_id=1, source_target_pairs={{0,2},{1,15},{2,4},{3,1},{4,6},{5,3},{6,8},{7,5},{8,10},{9,7},{10,... | collective-permute-start | bytes 1572872 | tf_op jit(solution)/shard_map/ppermute | solution.py:207
  117.2 4.4 %shard_map.61.refs_3_ = bf16[256,16,256]{2,1,0:T(8,128)(2,1)S(1)} custom-call(bf16[16,256,256]{2,1,0:T(8,128)(2,1)} %all-to-all-done.2.e_ref, bf16[256,256]{1,0:T(8,128)(2,1)S(1)} %get-tuple-element.95.p_ref), custom_call_target="tpu_custom_call" | custom-call | flops 1 | bytes 1 | tf_op jit(solution)/shard_map/pallas_call | solution.py:35
  121.7 4.5 %shard_map.62.refs_4_ = bf16[256,16,256]{2,1,0:T(8,128)(2,1)S(1)} custom-call(bf16[16,256,256]{2,1,0:T(8,128)(2,1)} %collective-permute-done.17.e_ref, bf16[256,256]{1,0:T(8,128)(2,1)S(1)} %get-tuple-element.93.p_ref), custom_call_target="tpu_custom_call" | custom-call | flops 1 | bytes 1 | tf_op jit(solution)/shard_map/pallas_call | solution.py:35
  126.2 2.7 %shard_map.63 = (f32[32,32]{1,0:T(8,128)S(1)}, f32[32,32]{1,0:T(8,128)S(1)}) custom-call(s32[7]{0:T(128)S(1)} %stack.46.refs_0_, bf16[256,16,256]{2,1,0:T(8,128)(2,1)S(1)} %shard_map.58.refs_1_, bf16[256,16,256]{2,1,0:T(8,128)(2,1)S(1)} %copy-done.3, bf16[256,16,256]{2,1,0:T(8,128)(2,1)S(1)} %shard_map.61.refs_3_, ...), custom_call_target="tpu_custom_call" | custom-call | flops 150994944 | bytes 9437184 | tf_op jit(solution)/shard_map/pallas_call | solution.py:124
  130.3 6.5 %all-to-all-start.3 = ((f32[32,8,128]{2,1,0:T(8,128)}), f32[32,8,128]{2,1,0:T(8,128)S(1)}, u32[]{:S(2)}, u32[]{:S(2)}) async-start(f32[32,8,128]{2,1,0:T(8,128)} %bitcast.24), calls=%async_computation.3 | async-start | bytes 262144 | tf_op jit(solution)/shard_map/all_to_all | solution.py:220
  137.6 6.9 %all-to-all-done.3 = f32[32,8,128]{2,1,0:T(8,128)S(1)} async-done(((f32[32,8,128]{2,1,0:T(8,128)}), f32[32,8,128]{2,1,0:T(8,128)S(1)}, u32[]{:S(2)}, u32[]{:S(2)}) %all-to-all-start.3) | async-done | bytes 131104 | tf_op jit(solution)/shard_map/all_to_all | solution.py:220
  (87 shorter events, 23.8 us)
Async XLA Ops:
  0.0 117.2 %copy-start = (s32[2048,2]{0,1:T(2,128)S(1)}, s32[2048,2]{0,1:T(2,128)}, u32[]{:S(2)}) copy-start(s32[2048,2]{0,1:T(2,128)} %param.8) | copy-start | bytes 49156
  0.0 7.2 %collective-permute-start = (bf16[8,2,256,256]{3,2,1,0:T(8,128)(2,1)}, bf16[8,2,256,256]{3,2,1,0:T(8,128)(2,1)S(1)}, u32[]{:S(2)}, u32[]{:S(2)}) collective-permute-start(bf16[8,2,256,256]{3,2,1,0:T(8,128)(2,1)} %refs_0_.3), channel_id=1, source_target_pairs={{0,1},{1,0},{2,3},{3,2},{4,5},{5,4},{6,7},{7,6},{8,9},{9,8},{10,11... | collective-permute-start | bytes 6291464 | tf_op jit(solution)/shard_map/ppermute | solution.py:17
  3.2 1.6 %copy-start.4 = (bf16[8,2,256,256]{3,2,1,0:T(8,128)(2,1)S(1)}, bf16[8,2,256,256]{3,2,1,0:T(8,128)(2,1)}, u32[]{:S(2)}) copy-start(bf16[8,2,256,256]{3,2,1,0:T(8,128)(2,1)} %refs_0_.3) | copy-start | bytes 6291460
  4.8 3.7 %copy-start.15 = (s32[4]{0:T(128)S(1)}, s32[4]{0:T(128)}, u32[]{:S(2)}) copy-start(s32[4]{0:T(128)} %when_ref.1) | copy-start | bytes 52
  8.6 1.6 %copy-start.7 = (bf16[8,2,256,256]{3,2,1,0:T(8,128)(2,1)S(1)}, bf16[8,2,256,256]{3,2,1,0:T(8,128)(2,1)}, u32[]{:S(2)}) copy-start(bf16[8,2,256,256]{3,2,1,0:T(8,128)(2,1)} %copy-done.6) | copy-start | bytes 6291460
  11.0 10.8 %collective-permute-start.1 = (bf16[2,8,32,256]{3,2,1,0:T(8,128)(2,1)S(1)}, bf16[2,8,32,256]{3,2,1,0:T(8,128)(2,1)S(1)}, u32[]{:S(2)}, u32[]{:S(2)}) collective-permute-start(bf16[2,8,32,256]{3,2,1,0:T(8,128)(2,1)S(1)} %get-tuple-element.90), channel_id=1, source_target_pairs={{0,14},{2,0},{4,2},{6,4},{8,6},{10,8},{12,10},{14,12},{1,15},{3,1}... | collective-permute-start | bytes 786440 | tf_op jit(solution)/shard_map/ppermute | solution.py:17
  14.9 34.9 %all-to-all-start = ((bf16[16,256,256]{2,1,0:T(8,128)(2,1)}), bf16[16,256,256]{2,1,0:T(8,128)(2,1)}, u32[]{:S(2)}, u32[]{:S(2)}) async-start(bf16[16,256,256]{2,1,0:T(8,128)(2,1)} %bitcast.56), calls=%async_computation | async-start | bytes 4194304 | tf_op jit(solution)/shard_map/all_to_all | solution.py:166
  21.8 7.1 %collective-permute-start.2 = (bf16[2,8,32,256]{3,2,1,0:T(8,128)(2,1)S(1)}, bf16[2,8,32,256]{3,2,1,0:T(8,128)(2,1)S(1)}, u32[]{:S(2)}, u32[]{:S(2)}) collective-permute-start(bf16[2,8,32,256]{3,2,1,0:T(8,128)(2,1)S(1)} %dynamic-slice_add_fusion.3), channel_id=1, source_target_pairs={{0,14},{2,0},{4,2},{6,4},{8,6},{10,8},{12,10},{14,12},{1,15},{3,1}... | collective-permute-start | bytes 786440 | tf_op jit(solution)/shard_map/ppermute | solution.py:17
  23.8 7.6 %collective-permute-start.3 = (bf16[2,8,32,256]{3,2,1,0:T(8,128)(2,1)S(1)}, bf16[2,8,32,256]{3,2,1,0:T(8,128)(2,1)S(1)}, u32[]{:S(2)}, u32[]{:S(2)}) collective-permute-start(bf16[2,8,32,256]{3,2,1,0:T(8,128)(2,1)S(1)} %get-tuple-element.47), channel_id=1, source_target_pairs={{0,2},{2,4},{4,6},{6,8},{8,10},{10,12},{12,14},{14,0},{1,3},{3,5},... | collective-permute-start | bytes 786440 | tf_op jit(solution)/shard_map/ppermute | solution.py:17
  31.6 5.7 %collective-permute-start.4 = (bf16[2,8,32,256]{3,2,1,0:T(8,128)(2,1)S(1)}, bf16[2,8,32,256]{3,2,1,0:T(8,128)(2,1)S(1)}, u32[]{:S(2)}, u32[]{:S(2)}) collective-permute-start(bf16[2,8,32,256]{3,2,1,0:T(8,128)(2,1)S(1)} %get-tuple-element.50), channel_id=1, source_target_pairs={{0,14},{2,0},{4,2},{6,4},{8,6},{10,8},{12,10},{14,12},{1,15},{3,1}... | collective-permute-start | bytes 786440 | tf_op jit(solution)/shard_map/ppermute | solution.py:17
  32.0 6.8 %collective-permute-start.5 = (bf16[2,8,32,256]{3,2,1,0:T(8,128)(2,1)S(1)}, bf16[2,8,32,256]{3,2,1,0:T(8,128)(2,1)S(1)}, u32[]{:S(2)}, u32[]{:S(2)}) collective-permute-start(bf16[2,8,32,256]{3,2,1,0:T(8,128)(2,1)S(1)} %get-tuple-element.51), channel_id=1, source_target_pairs={{0,2},{2,4},{4,6},{6,8},{8,10},{10,12},{12,14},{14,0},{1,3},{3,5},... | collective-permute-start | bytes 786440 | tf_op jit(solution)/shard_map/ppermute | solution.py:17
  33.2 1.6 %copy-start.5 = (bf16[8,2,256,256]{3,2,1,0:T(8,128)(2,1)S(1)}, bf16[8,2,256,256]{3,2,1,0:T(8,128)(2,1)}, u32[]{:S(2)}) copy-start(bf16[8,2,256,256]{3,2,1,0:T(8,128)(2,1)} %refs_0_.3) | copy-start | bytes 6291460
  39.0 6.4 %collective-permute-start.6 = (bf16[2,8,32,256]{3,2,1,0:T(8,128)(2,1)S(1)}, bf16[2,8,32,256]{3,2,1,0:T(8,128)(2,1)}, u32[]{:S(2)}, u32[]{:S(2)}) collective-permute-start(bf16[2,8,32,256]{3,2,1,0:T(8,128)(2,1)S(1)} %get-tuple-element.56), channel_id=1, source_target_pairs={{0,14},{2,0},{4,2},{6,4},{8,6},{10,8},{12,10},{14,12},{1,15},{3,1}... | collective-permute-start | bytes 786440 | tf_op jit(solution)/shard_map/ppermute | solution.py:17
  39.3 6.8 %collective-permute-start.7 = (bf16[2,8,32,256]{3,2,1,0:T(8,128)(2,1)S(1)}, bf16[2,8,32,256]{3,2,1,0:T(8,128)(2,1)}, u32[]{:S(2)}, u32[]{:S(2)}) collective-permute-start(bf16[2,8,32,256]{3,2,1,0:T(8,128)(2,1)S(1)} %get-tuple-element.57), channel_id=1, source_target_pairs={{0,2},{2,4},{4,6},{6,8},{8,10},{10,12},{12,14},{14,0},{1,3},{3,5},... | collective-permute-start | bytes 786440 | tf_op jit(solution)/shard_map/ppermute | solution.py:17
  41.6 5.7 %collective-permute-start.8 = (bf16[2,256,256]{2,1,0:T(8,128)(2,1)S(1)}, bf16[2,256,256]{2,1,0:T(8,128)(2,1)S(1)}, u32[]{:S(2)}, u32[]{:S(2)}) collective-permute-start(bf16[2,256,256]{2,1,0:T(8,128)(2,1)S(1)} %get-tuple-element.91), channel_id=1, source_target_pairs={{0,1},{1,0},{2,3},{3,2},{4,5},{5,4},{6,7},{7,6},{8,9},{9,8},{10,11... | collective-permute-start | bytes 786440 | tf_op jit(solution)/shard_map/ppermute | solution.py:17
  49.8 35.6 %collective-permute-start.11 = (bf16[16,256,256]{2,1,0:T(8,128)(2,1)}, bf16[16,256,256]{2,1,0:T(8,128)(2,1)}, u32[]{:S(2)}, u32[]{:S(2)}) collective-permute-start(bf16[16,256,256]{2,1,0:T(8,128)(2,1)} %all-to-all-done.e_ref), channel_id=1, source_target_pairs={{0,1},{1,0},{2,3},{3,2},{4,5},{5,4},{6,7},{7,6},{8,9},{9,8},{10,11... | collective-permute-start | bytes 6291464 | tf_op jit(solution)/shard_map/ppermute | solution.py:17
  68.5 39.5 %all-to-all-start.2 = ((bf16[16,256,256]{2,1,0:T(8,128)(2,1)}), bf16[16,256,256]{2,1,0:T(8,128)(2,1)}, u32[]{:S(2)}, u32[]{:S(2)}) async-start(bf16[16,256,256]{2,1,0:T(8,128)(2,1)} %bitcast.4), calls=%async_computation.2 | async-start | bytes 4194304 | tf_op jit(solution)/shard_map/all_to_all | solution.py:189
  72.9 12.5 %collective-permute-start.9 = (bf16[32,32,256]{2,1,0:T(8,128)(2,1)S(1)}, bf16[32,32,256]{2,1,0:T(8,128)(2,1)S(1)}, u32[]{:S(2)}, u32[]{:S(2)}) collective-permute-start(bf16[32,32,256]{2,1,0:T(8,128)(2,1)S(1)} %bitcast.52), channel_id=1, source_target_pairs={{0,2},{2,4},{4,6},{6,8},{8,10},{10,12},{12,14},{14,0},{1,3},{3,5},... | collective-permute-start | bytes 1572872 | tf_op jit(solution)/shard_map/ppermute | solution.py:17
  73.3 12.2 %collective-permute-start.10 = (bf16[32,32,256]{2,1,0:T(8,128)(2,1)S(1)}, bf16[32,32,256]{2,1,0:T(8,128)(2,1)S(1)}, u32[]{:S(2)}, u32[]{:S(2)}) collective-permute-start(bf16[32,32,256]{2,1,0:T(8,128)(2,1)S(1)} %bitcast.53), channel_id=1, source_target_pairs={{0,14},{2,0},{4,2},{6,4},{8,6},{10,8},{12,10},{14,12},{1,15},{3,1}... | collective-permute-start | bytes 1572872 | tf_op jit(solution)/shard_map/ppermute | solution.py:17
  85.4 7.2 %copy-start.9 = (bf16[32,32,256]{2,1,0:T(8,128)(2,1)}, bf16[32,32,256]{2,1,0:T(8,128)(2,1)S(1)}, u32[]{:S(2)}) copy-start(bf16[32,32,256]{2,1,0:T(8,128)(2,1)S(1)} %collective-permute-done.9.refs_4_.refs_6_) | copy-start | bytes 1572868
  85.4 7.2 %copy-start.12 = (bf16[32,32,256]{2,1,0:T(8,128)(2,1)}, bf16[32,32,256]{2,1,0:T(8,128)(2,1)S(1)}, u32[]{:S(2)}) copy-start(bf16[32,32,256]{2,1,0:T(8,128)(2,1)S(1)} %collective-permute-done.10.refs_5_.refs_7_) | copy-start | bytes 1572868
  85.5 11.7 %collective-permute-start.12 = (bf16[32,32,256]{2,1,0:T(8,128)(2,1)S(1)}, bf16[32,32,256]{2,1,0:T(8,128)(2,1)}, u32[]{:S(2)}, u32[]{:S(2)}) collective-permute-start(bf16[32,32,256]{2,1,0:T(8,128)(2,1)S(1)} %collective-permute-done.9.refs_4_.refs_6_), channel_id=1, source_target_pairs={{0,2},{2,4},{4,6},{6,8},{8,10},{10,12},{12,14},{14,0},{1,3},{3,5},... | collective-permute-start | bytes 1572872 | tf_op jit(solution)/shard_map/ppermute | solution.py:17
  85.5 11.6 %collective-permute-start.13 = (bf16[32,32,256]{2,1,0:T(8,128)(2,1)S(1)}, bf16[32,32,256]{2,1,0:T(8,128)(2,1)}, u32[]{:S(2)}, u32[]{:S(2)}) collective-permute-start(bf16[32,32,256]{2,1,0:T(8,128)(2,1)S(1)} %collective-permute-done.10.refs_5_.refs_7_), channel_id=1, source_target_pairs={{0,14},{2,0},{4,2},{6,4},{8,6},{10,8},{12,10},{14,12},{1,15},{3,1}... | collective-permute-start | bytes 1572872 | tf_op jit(solution)/shard_map/ppermute | solution.py:17
  97.1 10.8 %collective-permute-start.14 = (bf16[32,32,256]{2,1,0:T(8,128)(2,1)}, bf16[32,32,256]{2,1,0:T(8,128)(2,1)S(1)}, u32[]{:S(2)}, u32[]{:S(2)}) collective-permute-start(bf16[32,32,256]{2,1,0:T(8,128)(2,1)} %collective-permute-done.12.refs_6_.refs_8_), channel_id=1, source_target_pairs={{0,2},{2,4},{4,6},{6,8},{8,10},{10,12},{12,14},{14,0},{1,3},{3,5},... | collective-permute-start | bytes 1572872 | tf_op jit(solution)/shard_map/ppermute | solution.py:17
  97.1 10.8 %collective-permute-start.15 = (bf16[32,32,256]{2,1,0:T(8,128)(2,1)}, bf16[32,32,256]{2,1,0:T(8,128)(2,1)}, u32[]{:S(2)}, u32[]{:S(2)}) collective-permute-start(bf16[32,32,256]{2,1,0:T(8,128)(2,1)} %collective-permute-done.13.refs_7_.refs_9_), channel_id=1, source_target_pairs={{0,14},{2,0},{4,2},{6,4},{8,6},{10,8},{12,10},{14,12},{1,15},{3,1}... | collective-permute-start | bytes 1572872 | tf_op jit(solution)/shard_map/ppermute | solution.py:17
  99.9 1.6 %copy-start.2 = (bf16[256,16,256]{2,1,0:T(8,128)(2,1)S(1)}, bf16[256,16,256]{2,1,0:T(8,128)(2,1)}, u32[]{:S(2)}) copy-start(bf16[256,16,256]{2,1,0:T(8,128)(2,1)} %copy-done.1) | copy-start | bytes 6291460
  107.9 13.7 %collective-permute-start.17 = (bf16[16,256,256]{2,1,0:T(8,128)(2,1)}, bf16[16,256,256]{2,1,0:T(8,128)(2,1)}, u32[]{:S(2)}, u32[]{:S(2)}) collective-permute-start(bf16[16,256,256]{2,1,0:T(8,128)(2,1)} %all-to-all-done.2.e_ref), channel_id=1, source_target_pairs={{0,1},{1,0},{2,3},{3,2},{4,5},{5,4},{6,7},{7,6},{8,9},{9,8},{10,11... | collective-permute-start | bytes 6291464 | tf_op jit(solution)/shard_map/ppermute | solution.py:17
  114.1 14.9 %collective-permute-start.16 = (bf16[32,32,256]{2,1,0:T(8,128)(2,1)S(1)}, bf16[32,32,256]{2,1,0:T(8,128)(2,1)S(1)}, u32[]{:S(2)}, u32[]{:S(2)}) collective-permute-start(bf16[32,32,256]{2,1,0:T(8,128)(2,1)S(1)} %broadcast_select_fusion), channel_id=1, source_target_pairs={{0,2},{1,15},{2,4},{3,1},{4,6},{5,3},{6,8},{7,5},{8,10},{9,7},{10,... | collective-permute-start | bytes 1572872 | tf_op jit(solution)/shard_map/ppermute | solution.py:207
  121.6 4.6 %copy-start.3 = (bf16[256,16,256]{2,1,0:T(8,128)(2,1)S(1)}, bf16[256,16,256]{2,1,0:T(8,128)(2,1)}, u32[]{:S(2)}) copy-start(bf16[256,16,256]{2,1,0:T(8,128)(2,1)} %copy-done.1) | copy-start | bytes 6291460
  121.6 4.6 %copy-start.11 = (bf16[32,32,256]{2,1,0:T(8,128)(2,1)S(1)}, bf16[32,32,256]{2,1,0:T(8,128)(2,1)}, u32[]{:S(2)}) copy-start(bf16[32,32,256]{2,1,0:T(8,128)(2,1)} %copy-done.9) | copy-start | bytes 1572868
  121.6 4.6 %copy-start.14 = (bf16[32,32,256]{2,1,0:T(8,128)(2,1)S(1)}, bf16[32,32,256]{2,1,0:T(8,128)(2,1)}, u32[]{:S(2)}) copy-start(bf16[32,32,256]{2,1,0:T(8,128)(2,1)} %copy-done.12) | copy-start | bytes 1572868
  130.3 14.2 %all-to-all-start.3 = ((f32[32,8,128]{2,1,0:T(8,128)}), f32[32,8,128]{2,1,0:T(8,128)S(1)}, u32[]{:S(2)}, u32[]{:S(2)}) async-start(f32[32,8,128]{2,1,0:T(8,128)} %bitcast.24), calls=%async_computation.3 | async-start | bytes 262144 | tf_op jit(solution)/shard_map/all_to_all | solution.py:220
  (5 other events, 6.1 us)
